TPU v7x, 256 devices: a whole 4x4x8 slice. The times are simulated.
256 devices in a mesh: rep: 8 (over z), exp: 32 (over x, y, core).
Axes of the slice: x: 4, y: 4, z: 8, core: 2. Of those that a mesh axis runs over, the one named last changes fastest.
Arguments:
- tokens: bfloat16 [8, 4096, 4096], P('rep', 'exp'), may hold values from -6 to 6
- grad_out: bfloat16 [8, 4096, 4096], P('rep', 'exp'), may hold values from -6 to 6
- gates: float32 [8, 2, 128], P('rep'), may hold values from 0.1 to 1
- chosen: int32 [8, 2, 128], P('rep'), may hold values from 0 to 4095, as said below
- w_in: bfloat16 [2, 4096, 8192], P(None, None, 'exp'), may hold values from -0.09375 to 0.09375
- w_out: bfloat16 [2, 8192, 4096], P(None, 'exp'), may hold values from -0.0625 to 0.0625
Outputs:
- d_tokens: bfloat16 [8, 4096, 4096], P('rep', 'exp')
- d_gates: float32 [8, 2, 128], P('rep')
- d_w_in: bfloat16 [2, 4096, 8192], P(None, 'rep', 'exp')
- d_w_out: bfloat16 [2, 8192, 4096], P(None, 'exp', 'rep')
Inputs may be any that keep to these rules, and one draw needn't show every extreme that they name: `chosen`: each expert's list in a replica group holds 128 distinct token numbers; at most 8 of them lie among the 128 tokens of one device, and for every expert some device holds exactly 8.
All inputs are finite; a program needn't handle non-finite values.
Results may differ from a plain program's by a relative error of at most 0.02.
Values may be sent and summed in bfloat16 or wider, within the bound.
A program may use at most 192 MiB of HBM per device.

v0:
```python
import jax
import jax.numpy as jnp
from jax import lax
from jax.sharding import PartitionSpec as P

GELU_SCALE = 0.7978845608028654
GELU_CUBIC = 0.044715


def gelu_parts(hidden):
    tangent = jnp.tanh(GELU_SCALE * (hidden + GELU_CUBIC * hidden * hidden * hidden))
    activated = 0.5 * hidden * (1.0 + tangent)
    slope = 0.5 * (1.0 + tangent) + 0.5 * hidden * (1.0 - tangent * tangent) * GELU_SCALE * (
        1.0 + 3.0 * GELU_CUBIC * hidden * hidden
    )
    return (activated, slope)


def local(tokens, grad_out, gates, chosen, w_in, w_out):
    group_count = lax.axis_size("exp")
    my_index = lax.axis_index("exp")
    tok_dev = tokens.shape[1]
    model_width = tokens.shape[2]
    experts = chosen.shape[1]
    capacity = chosen.shape[2]
    most_rows = 2 * capacity // group_count
    padded_rows = group_count * experts * most_rows
    chosen_list = chosen[0]
    gate_list = gates[0]
    owner_dev = chosen_list // tok_dev
    local_row = chosen_list % tok_dev
    owner_hit = (
        owner_dev[:, :, None] == jnp.arange(group_count, dtype=jnp.int32)[None, None, :]
    ).astype(jnp.int32)
    slot_rank = jnp.sum((jnp.cumsum(owner_hit, axis=1) - 1) * owner_hit, axis=2)
    position = (
        owner_dev * (experts * most_rows)
        + jnp.arange(experts, dtype=jnp.int32)[:, None] * most_rows
        + slot_rank
    )
    flat_position = position.reshape(-1)
    is_mine = owner_dev == my_index
    selection = (
        is_mine[:, None, :]
        & (slot_rank[:, None, :] == jnp.arange(most_rows, dtype=jnp.int32)[None, :, None])
    ).astype(jnp.int32)
    slot_token = jnp.sum(selection * local_row[:, None, :], axis=2).reshape(-1)
    filled = jnp.sum(selection, axis=2).reshape(-1)
    picker = (slot_token[:, None] == jnp.arange(tok_dev, dtype=jnp.int32)[None, :]) & (
        filled[:, None] > 0
    )
    picker_bf = picker.astype(jnp.bfloat16)
    x_pack = jnp.dot(picker_bf, tokens[0], preferred_element_type=jnp.float32).astype(jnp.bfloat16)
    d_pack = jnp.dot(picker_bf, grad_out[0], preferred_element_type=jnp.float32).astype(
        jnp.bfloat16
    )
    x_all, d_all = (
        lax.all_gather(x_pack, "exp", axis=0, tiled=True),
        lax.all_gather(d_pack, "exp", axis=0, tiled=True),
    )
    x_rows = x_all.reshape(group_count, experts, most_rows, model_width)
    d_rows = d_all.reshape(group_count, experts, most_rows, model_width)
    gate_rows = (
        jnp.zeros((padded_rows,), jnp.float32)
        .at[flat_position]
        .set(gate_list.reshape(-1))
        .reshape(group_count, experts, most_rows)
    )
    hidden = jnp.einsum("oemd,edf->oemf", x_rows, w_in, preferred_element_type=jnp.float32)
    activated, slope = gelu_parts(hidden)
    activated = activated.astype(jnp.bfloat16)
    back_proj = jnp.einsum("oemd,efd->oemf", d_rows, w_out, preferred_element_type=jnp.float32)
    gate_part = jnp.sum(activated.astype(jnp.float32) * back_proj, axis=3)
    scaled = (gate_rows[..., None] * d_rows.astype(jnp.float32)).astype(jnp.bfloat16)
    d_hidden = (gate_rows[..., None] * back_proj * slope).astype(jnp.bfloat16)
    slot_grad = jnp.einsum("oemf,edf->oemd", d_hidden, w_in, preferred_element_type=jnp.float32)
    gate_slot = jnp.take(gate_part.reshape(-1), flat_position).reshape(experts, capacity)
    back_pad = slot_grad.reshape(padded_rows, model_width)
    gate_total = lax.psum(gate_slot, "exp")
    returned = lax.psum_scatter(
        back_pad.astype(jnp.bfloat16), "exp", scatter_dimension=0, tiled=True
    ).astype(jnp.float32)
    d_tok = jnp.dot(
        picker.astype(jnp.float32).T,
        returned,
        precision=lax.Precision.HIGHEST,
        preferred_element_type=jnp.float32,
    ).astype(jnp.bfloat16)
    part_in = jnp.einsum("oemd,oemf->edf", x_rows, d_hidden, preferred_element_type=jnp.float32)
    part_out = jnp.einsum("oemf,oemd->efd", activated, scaled, preferred_element_type=jnp.float32)
    grad_in, grad_out_proj = (
        lax.psum_scatter(
            part_in.astype(jnp.bfloat16), "rep", scatter_dimension=1, tiled=True
        ).astype(jnp.float32),
        lax.psum_scatter(
            part_out.astype(jnp.bfloat16), "rep", scatter_dimension=2, tiled=True
        ).astype(jnp.float32),
    )
    return (
        d_tok[None],
        gate_total[None],
        grad_in.astype(jnp.bfloat16),
        grad_out_proj.astype(jnp.bfloat16),
    )


def solution(mesh):
    return jax.shard_map(
        local,
        mesh=mesh,
        in_specs=(
            P("rep", "exp", None),
            P("rep", "exp", None),
            P("rep", None, None),
            P("rep", None, None),
            P(None, None, "exp"),
            P(None, "exp", None),
        ),
        out_specs=(
            P("rep", "exp", None),
            P("rep", None, None),
            P(None, "rep", "exp"),
            P(None, "exp", "rep"),
        ),
        check_vma=False,
    )
```

profile of v0, /device:TPU:1, one launch (start us, length us, event | category | flops | bytes accessed | tf_op | source)
XLA Modules:
  0.0 339.5 jit_solution(4204729013130801688)
XLA Ops:
  7.2 0.8 and_select_fusion.2
  8.0 0.7 broadcast_compare_fusion.1
  8.7 0.1 fusion.31
  8.8 0.2 reduce_window_sum.11
  9.0 0.2 select_reduce_fusion
  9.2 0.2 convert_reduce_fusion
  9.3 0.1 gt.12
  9.4 0.1 eq.61
  9.5 1.0 convolution_convert_fusion.2
  10.5 0.0 all-gather.3.cloned.1.call-start
  10.5 2.2 convolution_convert_fusion.3
  12.8 0.0 reduce-scatter.4.cloned.1.call-start
  12.8 0.1 add.118
  12.9 0.7 compare_select_fusion
  13.6 1.6 scatter_custom_fusion
  15.1 0.1 mul.118
  15.3 51.2 %all-gather.5.cloned.1.call-done = bf16[512,4096]{1,0:T(8,128)(2,1)} async-done(((bf16[16,4096]{1,0:T(8,128)(2,1)}), bf16[512,4096]{1,0:T(8,128)(2,1)}) %all-gather.5.cloned.1.call-update) | async-done | bytes 4194320 | tf_op jit(solution)/shard_map/all_gather | solution.py:58
  66.5 4.7 %fusion.16 = f32[32,2,8,256]{3,2,0,1:T(8,128)S(1)} fusion(bf16[2,4096,256]{2,1,0:T(8,128)(2,1)} %param.10, bf16[32,2,8,4096]{3,2,1,0:T(8,128)(2,1)} %bitcast.82), kind=kOutput, calls=%fused_computation.21 | convolution fusion | flops 1073741824 | bytes 8912896 | tf_op jit(solution)/shard_map/oemd,edf->oemf/dot_general | solution.py:69
  71.2 49.0 %all-gather.3.cloned.1.call-done = bf16[512,4096]{1,0:T(8,128)(2,1)} async-done(((bf16[16,4096]{1,0:T(8,128)(2,1)}), bf16[512,4096]{1,0:T(8,128)(2,1)}) %all-gather.3.cloned.1.call-update) | async-done | bytes 4194320 | tf_op jit(solution)/shard_map/all_gather | solution.py:59
  120.2 5.2 %multiply_reduce_fusion = (f32[32,2,8]{2,0,1:T(8,128)S(1)}, bf16[32,2,8,256]{3,2,0,1:T(8,128)(2,1)S(1)}) fusion(f32[32,2,8,256]{3,2,0,1:T(8,128)S(1)} %fusion.16, f32[32,2,8]{2,0,1:T(8,128)S(1)} %copy.34, bf16[2,256,4096]{2,1,0:T(8,128)(2,1)} %param.11, bf16[32,2,8,4096]{3,2,1,0:T(8,128)(2,1)} %bitcast.80), kind=kOutput, calls=%fused_computation.33 | convolution fusion | flops 1077018112 | bytes 9179136 | tf_op jit(solution)/shard_map/oemd,efd->oemf/dot_general | solution.py:72
  125.4 1.3 fusion
  126.7 2.5 copy.37
  129.2 5.9 %bitcast_convert_fusion.1 = bf16[2,4096,256]{2,1,0:T(8,128)(2,1)} fusion(bf16[32,2,8,4096]{3,2,1,0:T(8,128)(2,1)} %bitcast.83, bf16[32,2,8,256]{3,2,0,1:T(8,128)(2,1)S(1)} %get-tuple-element.9), kind=kOutput, calls=%fused_computation.3 | convolution fusion | flops 1075838976 | bytes 8650752 | tf_op jit(solution)/shard_map/oemd,oemf->edf/dot_general | solution.py:89
  135.2 5.6 %bitcast_convert_fusion = bf16[2,256,4096]{2,1,0:T(8,128)(2,1)} fusion(f32[32,2,8]{2,0,1:T(8,128)S(1)} %copy.34, bf16[32,2,8,4096]{3,2,1,0:T(8,128)(2,1)} %bitcast.81, f32[32,2,8,256]{3,2,0,1:T(8,128)S(1)} %fusion.16), kind=kOutput, calls=%fused_computation.2 | convolution fusion | flops 1083310080 | bytes 8914944 | tf_op jit(solution)/shard_map/oemf,oemd->efd/dot_general | solution.py:90
  140.9 0.1 reshape.235
  141.0 2.0 gather_fusion
  143.0 0.1 fusion.43
  143.1 63.1 %psum.7 = f32[1,2,128]{2,1,0:T(2,128)} all-reduce(f32[1,2,128]{2,1,0:T(2,128)S(1)} %fusion.43), channel_id=1, replica_groups=mesh['rep'=8,'exp'=32] {'exp'}, use_global_device_ids=true, to_apply=%region_7.8 | all-reduce | flops 256 | bytes 2048 | tf_op jit(solution)/shard_map/psum | solution.py:79
  206.1 10.2 %reduce-scatter.4.cloned.1.call-done = bf16[16,4096]{1,0:T(8,128)(2,1)} async-done(((bf16[512,4096]{1,0:T(8,128)(2,1)}), bf16[16,4096]{1,0:T(8,128)(2,1)}) %reduce-scatter.4.cloned.1.call-update) | async-done | bytes 131088 | tf_op jit(solution)/shard_map/reduce_scatter | solution.py:80
  216.4 2.4 fusion.1
  218.8 57.1 %reduce-scatter.6.cloned.1.call-done = bf16[2,512,256]{2,1,0:T(8,128)(2,1)} async-done(((bf16[2,4096,256]{2,1,0:T(8,128)(2,1)}), bf16[2,512,256]{2,1,0:T(8,128)(2,1)}) %reduce-scatter.6.cloned.1.call-update) | async-done | bytes 524304 | tf_op jit(solution)/shard_map/reduce_scatter | solution.py:92
  275.9 57.1 %reduce-scatter.8.cloned.1.call-done = bf16[2,256,512]{2,1,0:T(8,128)(2,1)} async-done(((bf16[2,256,4096]{2,1,0:T(8,128)(2,1)}), bf16[2,256,512]{2,1,0:T(8,128)(2,1)}) %reduce-scatter.8.cloned.1.call-update) | async-done | bytes 524304 | tf_op jit(solution)/shard_map/reduce_scatter | solution.py:95
  (17 shorter events, 0.3 us)
Async XLA Ops:
  7.2 2.3 copy-start
  7.2 59.3 %all-gather.5.cloned.1.call-start = ((), (), s32[]{:S(2)}) async-start(), calls=%async_computation.4 | async-start | bytes 4325376 | tf_op jit(solution)/shard_map/all_gather | solution.py:58
  10.5 109.7 %all-gather.3.cloned.1.call-start = ((), (), s32[]{:S(2)}) async-start(), calls=%async_computation.3 | async-start | bytes 4325376 | tf_op jit(solution)/shard_map/all_gather | solution.py:59
  12.8 203.6 %reduce-scatter.4.cloned.1.call-start = ((), (), s32[]{:S(2)}) async-start(), calls=%async_computation.5 | async-start | bytes 4325376 | tf_op jit(solution)/shard_map/reduce_scatter | solution.py:80
  120.2 5.2 %copy-start.1 = (bf16[2,4096,256]{2,1,0:T(8,128)(2,1)S(1)}, bf16[2,4096,256]{2,1,0:T(8,128)(2,1)}, u32[]{:S(2)}) copy-start(bf16[2,4096,256]{2,1,0:T(8,128)(2,1)} %param.10) | copy-start | bytes 12582916
  129.2 146.7 %reduce-scatter.6.cloned.1.call-start = ((), (), s32[]{:S(2)}) async-start(), calls=%async_computation.6 | async-start | bytes 4718592 | tf_op jit(solution)/shard_map/reduce_scatter | solution.py:92
  135.2 197.8 %reduce-scatter.8.cloned.1.call-start = ((), (), s32[]{:S(2)}) async-start(), calls=%async_computation.7 | async-start | bytes 4718592 | tf_op jit(solution)/shard_map/reduce_scatter | solution.py:95
Sparse Core Ops, SparseCore 0:
  11.1 55.2 all-gather.4
  69.6 50.5 all-gather.2
  129.3 87.0 reduce-scatter.3
  219.5 56.3 reduce-scatter.5
  279.0 53.9 reduce-scatter.7
where the time goes:
time: 340 us
  waiting for transfers between devices  225 us (66%)
  blocking collectives  63.1 us (19%)
  matrix products  28.3 us (8%)
  between operations  13.9 us (4%)
  local copies, waits for them, and re-layouts  6.46 us (2%)
    psum x1, blocking collectives, local(): gate_total = lax.psum(gate_slot, 'exp')  63.1 us
    reduce_scatter x1, waiting for transfers between devices, local(): lax.psum_scatter(part_in.astype(jnp.bfloat16), 'rep', scatter_dimension=1...  57.1 us
    reduce_scatter x1, waiting for transfers between devices, local(): lax.psum_scatter(part_out.astype(jnp.bfloat16), 'rep', scatter_dimension=...  57.1 us
    all_gather x1, waiting for transfers between devices, local(): lax.all_gather(x_pack, 'exp', axis=0, tiled=True)  51.2 us
    all_gather x1, waiting for transfers between devices, local(): lax.all_gather(d_pack, 'exp', axis=0, tiled=True)  49 us
    reduce_scatter x1, waiting for transfers between devices, local(): lax.psum_scatter(back_pad.astype(jnp.bfloat16), 'exp', scatter_dimension=...  10.2 us
  transfers between devices with their start and end apart: 5, of which 5 were waited for; matrix products, arithmetic and copies ran while one was open for 7% of the time, Pallas kernels for 0%

commit v1 on v0

v1 whole, which is shorter than its diff:
```python
import functools

import jax
import jax.numpy as jnp
from jax import lax
from jax.experimental import pallas as pl
from jax.experimental.pallas import tpu as pltpu
from jax.sharding import PartitionSpec as P

GELU_SCALE = 0.7978845608028654
GELU_CUBIC = 0.044715

BF = jnp.bfloat16
F32 = jnp.float32
MESH = pl.DeviceIdType.MESH

NX, NY, NZ = 4, 4, 8
D = 4096
F = 256
CAP = 128
TOK = 128
MOST = 8
ROWS = 2 * MOST
PAD = NX * NY * 2 * ROWS
HALF = D // 2
DS_W = D // NZ
BLK = 512

NSEM = 96


def dot(a, b, ca=1, cb=0):
    return lax.dot_general(a, b, (((ca,), (cb,)), ((), ())), preferred_element_type=F32)


def kernel(
    tok_hbm, grad_hbm, gates_ref, chosen_ref, win_hbm, wout_hbm,
    dtok_ref, dgate_ref, dwin_ref, dwout_ref,
    tok, grad, win, wout, xg, dg, cc, ds, zb, acc, ps, rsib, rs1, ts, rs2, gbuf, gsib, gx, gy,
    ssem, rsem, lsem,
):
    r = lax.axis_index("rep")
    e = lax.axis_index("exp")
    x = e // 8
    y = (e // 2) % 4
    c = e % 2
    oc = 1 - c

    def dev(rr, xx, yy, c_):
        return (rr, (xx * 4 + yy) * 2 + c_)

    def xs(d):
        return lax.rem(x + d, 4)

    def ys(d):
        return lax.rem(y + d, 4)

    def zs(d):
        return lax.rem(r + d, 8)

    sib = dev(r, x, y, oc)

    loads = [
        pltpu.make_async_copy(tok_hbm.at[0], tok, lsem.at[0]),
        pltpu.make_async_copy(grad_hbm.at[0], grad, lsem.at[1]),
        pltpu.make_async_copy(win_hbm, win, lsem.at[2]),
        pltpu.make_async_copy(wout_hbm, wout, lsem.at[3]),
    ]
    for load in loads:
        load.start()

    barrier = pltpu.get_barrier_semaphore()
    partners = (
        [sib]
        + [dev(r, xs(d), y, c) for d in (1, 2, 3)]
        + [dev(r, x, ys(d), c) for d in (1, 2, 3)]
        + [dev(zs(d), x, y, c) for d in range(1, 8)]
    )
    for p in partners:
        pl.semaphore_signal(barrier, inc=1, device_id=p, device_id_type=MESH)

    counter = [0]
    sent = []

    def send(src, dst, to):
        i = counter[0]
        counter[0] += 1
        cp = pltpu.make_async_remote_copy(
            src_ref=src, dst_ref=dst, send_sem=ssem.at[i], recv_sem=rsem.at[i],
            device_id=to, device_id_type=MESH,
        )
        cp.start()
        sent.append(cp)
        return cp

    def iota(shape, dim):
        return lax.broadcasted_iota(jnp.int32, shape, dim)

    sq = (CAP, CAP)
    ch_row, ch_col, pos_row, pos_col, gate_col = [], [], [], [], []
    for k in range(2):
        row = chosen_ref[0, k : k + 1, :]
        rb = jnp.broadcast_to(row, sq)
        cb = rb.T
        ob_row, ob_col = rb // TOK, cb // TOK
        same = (ob_row == ob_col)
        before_row = jnp.where(same & (iota(sq, 1) < iota(sq, 0)), 1, 0)
        before_col = jnp.where(same & (iota(sq, 0) < iota(sq, 1)), 1, 0)
        rank_col = jnp.sum(before_row, axis=1, keepdims=True)
        rank_row = jnp.sum(before_col, axis=0, keepdims=True)

        def place(own, rank):
            return ((own % 2) * (NX * NY) + own // 2) * ROWS + k * MOST + rank

        ch_row.append(row)
        ch_col.append(cb[:, 0:1])
        pos_row.append(place(row // TOK, rank_row))
        pos_col.append(place(cb[:, 0:1] // TOK, rank_col))
        gate_col.append(jnp.broadcast_to(gates_ref[0, k : k + 1, :], sq).T[:, 0:1])

    my_first = (c * (NX * NY) + x * NY + y) * ROWS

    def hot(m):
        return jnp.where(m, 1.0, 0.0).astype(BF)

    pick = jnp.zeros((ROWS, TOK), F32)
    unpick = jnp.zeros((TOK, 2 * ROWS), F32)
    for k in range(2):
        a = hot(pos_row[k] - my_first == iota((ROWS, CAP), 0))
        b = hot(ch_col[k] - e * TOK == iota((CAP, TOK), 1))
        pick += dot(a, b)
        bt = hot(ch_row[k] - e * TOK == iota((TOK, CAP), 0))
        at = hot(pos_col[k] - my_first == iota((CAP, 2 * ROWS), 1) % ROWS)
        unpick += dot(bt, at)
    pick = pick.astype(BF)
    unpick = unpick.astype(BF)
    expand = [hot(pos_row[k] == iota((PAD, CAP), 0)) for k in range(2)]
    gather = jnp.concatenate([hot(pos_col[k] == iota((CAP, PAD), 1)) for k in range(2)], axis=0)

    loads[0].wait()
    loads[1].wait()

    @pl.loop(0, D // BLK)
    def _(j):
        cols = pl.ds(pl.multiple_of(j * BLK, BLK), BLK)
        xg[c, x, y, :, cols] = dot(pick, tok[:, cols]).astype(BF)
        dg[c, x, y, :, cols] = dot(pick, grad[:, cols]).astype(BF)

    pl.semaphore_wait(barrier, len(partners))

    p1 = []
    for d in (1, 3, 2):
        p1.append(send(xg.at[c, x, y], xg.at[c, x, y], dev(r, xs(d), y, c)))
        p1.append(send(dg.at[c, x, y], dg.at[c, x, y], dev(r, x, ys(d), c)))
    for cp in p1:
        cp.wait_recv()
    up_x = send(xg.at[c, :, y], xg.at[c, :, y], dev(r, x, ys(1), c))
    up_d = send(dg.at[c, x], dg.at[c, x], dev(r, xs(1), y, c))
    dn_x = send(xg.at[c, :, y], xg.at[c, :, y], dev(r, x, ys(3), c))
    dn_d = send(dg.at[c, x], dg.at[c, x], dev(r, xs(3), y, c))
    sibs = [send(xg.at[c, :, y], xg.at[c, :, y], sib), send(dg.at[c, x], dg.at[c, x], sib)]
    loads[2].wait()
    loads[3].wait()
    up_x.wait_recv()
    fw = [send(xg.at[c, 0:2, ys(3)], xg.at[c, 0:2, ys(3)], dev(r, x, ys(1), c))]
    up_d.wait_recv()
    fw.append(send(dg.at[c, xs(3), 0:2], dg.at[c, xs(3), 0:2], dev(r, xs(1), y, c)))
    dn_x.wait_recv()
    fw.append(send(xg.at[c, 2:4, ys(1)], xg.at[c, 2:4, ys(1)], dev(r, x, ys(3), c)))
    dn_d.wait_recv()
    fw.append(send(dg.at[c, xs(1), 2:4], dg.at[c, xs(1), 2:4], dev(r, xs(3), y, c)))
    for d in (1, 3):
        sibs.append(send(xg.at[c, :, ys(d)], xg.at[c, :, ys(d)], sib))
        sibs.append(send(dg.at[c, xs(d)], dg.at[c, xs(d)], sib))
    for cp in fw:
        cp.wait_recv()
    sibs.append(send(xg.at[c, :, ys(2)], xg.at[c, :, ys(2)], sib))
    sibs.append(send(dg.at[c, xs(2)], dg.at[c, xs(2)], sib))
    for cp in sibs:
        cp.wait_recv()

    acc[...] = jnp.zeros_like(acc)
    gcol = jnp.concatenate(gate_col, axis=0)

    @pl.loop(0, D // BLK)
    def _(j):
        cols = pl.ds(pl.multiple_of(j * BLK, BLK), BLK)
        xc = dot(gather, xg[:, :, :, :, cols].reshape(PAD, BLK)).astype(BF)
        dc = dot(gather, dg[:, :, :, :, cols].reshape(PAD, BLK))
        cc[0, :, :, cols] = xc.reshape(NX * NY, ROWS, BLK)
        cc[1, :, :, cols] = (gcol * dc).astype(BF).reshape(NX * NY, ROWS, BLK)
        dc = dc.astype(BF)
        for k in range(2):
            sl = slice(k * CAP, (k + 1) * CAP)
            acc[0, k] += dot(xc[sl], win[k, cols, :])
            acc[1, k] += dot(dc[sl], wout[k, :, cols], 1, 1)

    dpad = []
    for k in range(2):
        hidden = acc[0, k]
        back = acc[1, k]
        tang = jnp.tanh(GELU_SCALE * (hidden + GELU_CUBIC * hidden * hidden * hidden))
        act = (0.5 * hidden * (1.0 + tang)).astype(BF)
        slope = 0.5 * (1.0 + tang) + 0.5 * hidden * (1.0 - tang * tang) * GELU_SCALE * (
            1.0 + 3.0 * GELU_CUBIC * hidden * hidden
        )
        dh = (gate_col[k] * back * slope).astype(BF)
        zb[r, 0, k] = act
        zb[r, 1, k] = dh
        gbuf[0, k] = lax.dot_general(
            jnp.ones((8, F), F32), act.astype(F32) * back, (((1,), (1,)), ((), ())),
            precision=lax.Precision.HIGHEST, preferred_element_type=F32,
        )
        dpad.append(dot(expand[k], dh).astype(BF))

    right, left = dev(zs(1), x, y, c), dev(zs(7), x, y, c)
    zr = send(zb.at[r], zb.at[r], right)
    zl = send(zb.at[r], zb.at[r], left)

    chip = x * NY + y
    own_ds = pltpu.make_async_copy(
        cc.at[c, chip, :, pl.ds(pl.multiple_of(r * DS_W, DS_W), DS_W)], ds.at[c, r, x, y], lsem.at[0]
    )
    own_ds.start()
    ex = []
    for d in (1, 7, 2, 6, 3, 5, 4):
        cols = pl.ds(pl.multiple_of(zs(d) * DS_W, DS_W), DS_W)
        ex.append(send(cc.at[c, chip, :, cols], ds.at[c, r, x, y], dev(zs(d), x, y, c)))
    g0 = send(gbuf.at[0], gsib, sib)

    halves = []
    for h in range(2):

        @pl.loop(h * (HALF // BLK), (h + 1) * (HALF // BLK))
        def _(j):
            cols = pl.ds(pl.multiple_of(j * BLK, BLK), BLK)
            part = dot(dpad[0], win[0, cols, :], 1, 1) + dot(dpad[1], win[1, cols, :], 1, 1)
            ps[:, :, :, :, cols] = part.astype(BF).reshape(2, NX, NY, ROWS, BLK)

        hc = pl.ds(h * HALF, HALF)
        halves.append(send(ps.at[oc, :, :, :, hc], rsib.at[:, :, :, hc], sib))

    own_ds.wait()
    for cp in ex:
        cp.wait_recv()
    q1 = []
    for d in (1, 3, 2):
        q1.append(send(ds.at[c, 0:4, x, y], ds.at[c, 0:4, x, y], dev(r, xs(d), y, c)))
        q1.append(send(ds.at[c, 4:8, x, y], ds.at[c, 4:8, x, y], dev(r, x, ys(d), c)))

    g0.wait_recv()
    gbuf[1] = gbuf[0] + gsib[...]
    gx[x] = gbuf[1]
    g1 = [send(gbuf.at[1], gx.at[x], dev(r, xs(d), y, c)) for d in (1, 3, 2)]

    zr.wait_recv()
    zr = send(zb.at[zs(7)], zb.at[zs(7)], right)
    zl.wait_recv()
    zl = send(zb.at[zs(1)], zb.at[zs(1)], left)

    stage1 = []
    for h in range(2):
        halves[h].wait_recv()
        hc = pl.ds(h * HALF, HALF)

        @pl.loop(0, NX)
        def _(i):
            for j in range(NY):
                own = ps[c, i, j, :, hc].astype(F32)
                ps[c, i, j, :, hc] = (own + rsib[i, j, :, hc].astype(F32)).astype(BF)

        for d in (1, 3, 2):
            if h == 0:
                stage1.append(send(ps.at[c, xs(d), :, :, hc], rs1.at[0, x], dev(r, xs(d), y, c)))
            else:
                stage1.append(send(ps.at[c, :, ys(d), :, hc], rs1.at[1, y], dev(r, x, ys(d), c)))

    for cp in q1:
        cp.wait_recv()
    q2 = []
    for d in (1, 3, 2):
        q2.append(send(ds.at[c, 0:4, :, y], ds.at[c, 0:4, :, y], dev(r, x, ys(d), c)))
        q2.append(send(ds.at[c, 4:8, x], ds.at[c, 4:8, x], dev(r, xs(d), y, c)))

    zr.wait_recv()
    zr = send(zb.at[zs(6)], zb.at[zs(6)], right)
    zl.wait_recv()
    zl = send(zb.at[zs(2)], zb.at[zs(2)], left)

    for cp in g1:
        cp.wait_recv()
    gbuf[2] = (gx[0] + gx[1]) + (gx[2] + gx[3])
    gy[y] = gbuf[2]
    g2 = [send(gbuf.at[2], gy.at[y], dev(r, x, ys(d), c)) for d in (1, 3, 2)]

    stage2 = []
    for h in range(2):
        for cp in stage1[3 * h : 3 * h + 3]:
            cp.wait_recv()
        hc = pl.ds(h * HALF, HALF)
        for j in range(4):
            total = (ps[c, x, j, :, hc] if h == 0 else ps[c, j, y, :, hc]).astype(F32)
            for d in (1, 2, 3):
                total += rs1[h, xs(d) if h == 0 else ys(d), j].astype(F32)
            ts[h, j] = total.astype(BF)
        for d in (1, 3, 2):
            if h == 0:
                stage2.append(send(ts.at[0, ys(d)], rs2.at[0, y], dev(r, x, ys(d), c)))
            else:
                stage2.append(send(ts.at[1, xs(d)], rs2.at[1, x], dev(r, xs(d), y, c)))

    zr.wait_recv()
    zr = send(zb.at[zs(5), 0], zb.at[zs(5), 0], right)
    zl.wait_recv()
    zl = send(zb.at[zs(3), 1], zb.at[zs(3), 1], left)

    for cp in q2:
        cp.wait_recv()
    q3 = send(ds.at[c], ds.at[c], sib)

    for cp in g2:
        cp.wait_recv()
    total = (gy[0] + gy[1]) + (gy[2] + gy[3])
    for k in range(2):
        dgate_ref[0, k : k + 1, :] = total[k, 0:1, :]

    for h in range(2):
        for cp in stage2[3 * h : 3 * h + 3]:
            cp.wait_recv()
        total = ts[h, y if h == 0 else x].astype(F32)
        for d in (1, 2, 3):
            total += rs2[h, ys(d) if h == 0 else xs(d)].astype(F32)
        high = total.astype(BF)
        low = (total - high.astype(F32)).astype(BF)
        both = jnp.concatenate([high, low], axis=0)
        for j in range(HALF // BLK):
            dtok_ref[0, :, h * HALF + j * BLK : h * HALF + (j + 1) * BLK] = dot(
                unpick, both[:, j * BLK : (j + 1) * BLK]
            ).astype(BF)

    zr.wait_recv()
    zl.wait_recv()
    q3.wait_recv()
    for k in range(2):
        xk = ds[0, :, 2 * k : 2 * k + 2].reshape(NZ * CAP, DS_W)
        sk = ds[1, :, 2 * k : 2 * k + 2].reshape(NZ * CAP, DS_W)
        dwin_ref[k] = dot(xk, zb[:, 1, k].reshape(NZ * CAP, F), 0, 0).astype(BF)
        dwout_ref[k] = dot(zb[:, 0, k].reshape(NZ * CAP, F), sk, 0, 0).astype(BF)

    assert counter[0] <= NSEM, counter[0]
    for cp in sent:
        cp.wait_send()


def local(tokens, grad_out, gates, chosen, w_in, w_out):
    hbm = pl.BlockSpec(memory_space=pl.ANY)
    vmem = pl.BlockSpec(memory_space=pltpu.VMEM)
    return pl.pallas_call(
        kernel,
        out_shape=(
            jax.ShapeDtypeStruct((1, TOK, D), BF),
            jax.ShapeDtypeStruct((1, 2, CAP), F32),
            jax.ShapeDtypeStruct((2, DS_W, F), BF),
            jax.ShapeDtypeStruct((2, F, DS_W), BF),
        ),
        in_specs=[hbm, hbm, vmem, vmem, hbm, hbm],
        out_specs=(vmem, vmem, vmem, vmem),
        scratch_shapes=[
            pltpu.VMEM((TOK, D), BF),
            pltpu.VMEM((TOK, D), BF),
            pltpu.VMEM((2, D, F), BF),
            pltpu.VMEM((2, F, D), BF),
            pltpu.VMEM((2, NX, NY, ROWS, D), BF),
            pltpu.VMEM((2, NX, NY, ROWS, D), BF),
            pltpu.VMEM((2, NX * NY, ROWS, D), BF),
            pltpu.VMEM((2, NZ, NX, NY, ROWS, DS_W), BF),
            pltpu.VMEM((NZ, 2, 2, CAP, F), BF),
            pltpu.VMEM((2, 2, CAP, F), F32),
            pltpu.VMEM((2, NX, NY, ROWS, D), BF),
            pltpu.VMEM((NX, NY, ROWS, D), BF),
            pltpu.VMEM((2, 4, 4, ROWS, HALF), BF),
            pltpu.VMEM((2, 4, ROWS, HALF), BF),
            pltpu.VMEM((2, 4, ROWS, HALF), BF),
            pltpu.VMEM((3, 2, 8, CAP), F32),
            pltpu.VMEM((2, 8, CAP), F32),
            pltpu.VMEM((4, 2, 8, CAP), F32),
            pltpu.VMEM((4, 2, 8, CAP), F32),
            pltpu.SemaphoreType.DMA((NSEM,)),
            pltpu.SemaphoreType.DMA((NSEM,)),
            pltpu.SemaphoreType.DMA((4,)),
        ],
        compiler_params=pltpu.CompilerParams(
            collective_id=0, has_side_effects=True, vmem_limit_bytes=60 << 20
        ),
        name="expert_backward",
    )(tokens, grad_out, gates, chosen, w_in, w_out)


def solution(mesh):
    return jax.shard_map(
        local,
        mesh=mesh,
        in_specs=(
            P("rep", "exp", None),
            P("rep", "exp", None),
            P("rep", None, None),
            P("rep", None, None),
            P(None, None, "exp"),
            P(None, "exp", None),
        ),
        out_specs=(
            P("rep", "exp", None),
            P("rep", None, None),
            P(None, "rep", "exp"),
            P(None, "exp", "rep"),
        ),
        check_vma=False,
    )
```

time: 340 us -> 102 us (0.30)
  waiting for transfers between devices: 225 us -> 0 us
  Pallas kernels: 0 us -> 93.9 us
  blocking collectives: 63.1 us -> 0 us
  matrix products: 28.3 us -> 0 us
  between operations: 13.9 us -> 0.64 us
    reduce_scatter x3 -> x0, waiting for transfers between devices: 124 us -> none  [the longest x1 57.1 us: local(): lax.psum_scatter(part_in.astype(jnp.bfloat16), 'rep', scatter_dimension=1...]
    all_gather x2 -> x0, waiting for transfers between devices: 100 us -> none  [the longest x1 51.2 us: local(): lax.all_gather(x_pack, 'exp', axis=0, tiled=True)]
    pallas_call x0 -> x1, Pallas kernels: none -> 93.9 us  [local(): pl.pallas_call(kernel, out_shape=(jax.ShapeDtypeStruct((1, TOK, D), BF),...]
    psum x1 -> x0, blocking collectives: 63.1 us -> none  [local(): gate_total = lax.psum(gate_slot, 'exp')]
    dot_general x8 -> x0, matrix products: 28.3 us -> none  [the longest x1 5.91 us: local(): jnp.einsum('oemd,oemf->edf', x_rows, d_hidden, preferred_element_type=jnp...]
    unnamed x4, local copies, waits for them, and re-layouts: 0.01 us -> 7.25 us
  transfers between devices with their start and end apart: 5 -> 0, of which waited for: 5 -> 0; matrix products, arithmetic and copies ran while one was open for 7% -> 0% of each run, Pallas kernels for 0% -> 0%
where the time goes in v1:
time: 102 us
  Pallas kernels  93.9 us (92%)
  local copies, waits for them, and re-layouts  7.25 us (7%)
    pallas_call x1, Pallas kernels, local(): pl.pallas_call(kernel, out_shape=(jax.ShapeDtypeStruct((1, TOK, D), BF),...  93.9 us
    unnamed x4, local copies, waits for them, and re-layouts  7.25 us

profile of v1, /device:TPU:1, one launch (start us, length us, event | category | flops | bytes accessed | tf_op | source)
XLA Modules:
  0.0 101.8 jit_solution(12659855801538436918)
XLA Ops:
  0.6 93.9 %expert_backward.1 = (bf16[1,128,4096]{2,1,0:T(8,128)(2,1)}, f32[1,2,128]{2,1,0:T(2,128)}, bf16[2,512,256]{2,1,0:T(8,128)(2,1)}, bf16[2,256,512]{2,1,0:T(8,128)(2,1)}) custom-call(bf16[1,128,4096]{2,1,0:T(8,128)(2,1)} %tok_hbm.1, bf16[1,128,4096]{2,1,0:T(8,128)(2,1)} %grad_hbm.1, f32[1,2,128]{2,1,0:T(2,128)} %gates_ref.1, s32[1,2,128]{2,1,0:T(2,128)} %chosen_ref.1, ...), custom_call_target="tpu_custom_call" | custom-call | tf_op jit(solution)/shard_map/expert_backward/pallas_call | solution.py:358
  94.5 2.3 %copy.14 = bf16[1,128,4096]{2,1,0:T(8,128)(2,1)} copy(bf16[1,128,4096]{2,1,0:T(8,128)(2,1)} %get-tuple-element.8) | data formatting | bytes 2097152
  96.8 1.2 %copy.15 = f32[1,2,128]{2,1,0:T(2,128)} copy(f32[1,2,128]{2,1,0:T(2,128)} %get-tuple-element.9) | data formatting | bytes 2048
  98.0 1.9 %copy.16 = bf16[2,512,256]{2,1,0:T(8,128)(2,1)} copy(bf16[2,512,256]{2,1,0:T(8,128)(2,1)} %get-tuple-element.10) | data formatting | bytes 1048576
  99.9 1.9 %copy.17 = bf16[2,256,512]{2,1,0:T(8,128)(2,1)} copy(bf16[2,256,512]{2,1,0:T(8,128)(2,1)} %get-tuple-element.11) | data formatting | bytes 1048576

commit v2 on v1

v2 whole, which is shorter than its diff:
```python
import jax
import jax.numpy as jnp
from jax import lax
from jax.experimental import pallas as pl
from jax.experimental.pallas import tpu as pltpu
from jax.sharding import PartitionSpec as P

GELU_SCALE = 0.7978845608028654
GELU_CUBIC = 0.044715

BF = jnp.bfloat16
F32 = jnp.float32
MESH = pl.DeviceIdType.MESH

NX, NY, NZ = 4, 4, 8
D = 4096
F = 256
CAP = 128
TOK = 128
MOST = 8
ROWS = 2 * MOST
PAD = NX * NY * 2 * ROWS
COL = 128
BLK = D // NX
PLANE = NX * NY * 2

NSEM = 104


def dot(a, b, ca=1, cb=0):
    return lax.dot_general(a, b, (((ca,), (cb,)), ((), ())), preferred_element_type=F32)


def kernel(
    tok_hbm, grad_hbm, gates_ref, chosen_ref, win_hbm, wout_hbm,
    rows_ref, unpick_ref, dgate_ref, dwin_ref, dwout_ref,
    tok, grad, win, wout, pk, rp, xc, gc, eb, ds, zb, acc, ps, rsib, rs1, ts, rs2, ob, rb,
    gbuf, gsib, gx, gy,
    ssem, rsem, asem, arsem, bsem, brsem, lsem,
):
    r = lax.axis_index("rep")
    e = lax.axis_index("exp")
    x = e // 8
    y = (e // 2) % 4
    c = e % 2
    oc = 1 - c
    chip = x * NY + y

    def dev(rr, xx, yy, c_):
        return (rr, (xx * 4 + yy) * 2 + c_)

    def xs(d):
        return lax.rem(x + d, 4)

    def ys(d):
        return lax.rem(y + d, 4)

    def zs(d):
        return lax.rem(r + d, 8)

    sib = dev(r, x, y, oc)

    loads = [
        pltpu.make_async_copy(tok_hbm.at[0], tok, lsem.at[0]),
        pltpu.make_async_copy(grad_hbm.at[0], grad, lsem.at[1]),
        pltpu.make_async_copy(win_hbm, win, lsem.at[2]),
        pltpu.make_async_copy(wout_hbm, wout, lsem.at[3]),
    ]
    loads[0].start()
    loads[1].start()

    def partner(i):
        return lax.rem(x + i // 8, 4), lax.rem(y + (i // 2) % 4, 4), lax.rem(c + i, 2)

    barrier = pltpu.get_barrier_semaphore()

    @pl.loop(1, PLANE)
    def _(i):
        px, py, pc = partner(i)
        pl.semaphore_signal(barrier, inc=1, device_id=dev(r, px, py, pc), device_id_type=MESH)

    for d in range(1, NZ):
        pl.semaphore_signal(barrier, inc=1, device_id=dev(zs(d), x, y, c), device_id_type=MESH)

    counter = [0]
    sent = []

    def send(src, dst, to):
        i = counter[0]
        counter[0] += 1
        cp = pltpu.make_async_remote_copy(
            src_ref=src, dst_ref=dst, send_sem=ssem.at[i], recv_sem=rsem.at[i],
            device_id=to, device_id_type=MESH,
        )
        cp.start()
        sent.append(cp)
        return cp

    def iota(shape, dim):
        return lax.broadcasted_iota(jnp.int32, shape, dim)

    def hot(m):
        return jnp.where(m, 1.0, 0.0).astype(BF)

    sq = (CAP, CAP)
    my_first = (c * (NX * NY) + chip) * ROWS
    ch_row, ch_col, pos_row, pos_col, gate_col = [], [], [], [], []
    for k in range(2):
        row = chosen_ref[0, k : k + 1, :]
        rb_ = jnp.broadcast_to(row, sq)
        cb_ = rb_.T
        same = (rb_ // TOK) == (cb_ // TOK)
        rank_col = jnp.sum(jnp.where(same & (iota(sq, 1) < iota(sq, 0)), 1, 0), axis=1, keepdims=True)
        rank_row = jnp.sum(jnp.where(same & (iota(sq, 0) < iota(sq, 1)), 1, 0), axis=0, keepdims=True)

        def place(own, rank):
            return ((own % 2) * (NX * NY) + own // 2) * ROWS + k * MOST + rank

        ch_row.append(row)
        ch_col.append(cb_[:, 0:1])
        pos_row.append(place(row // TOK, rank_row))
        pos_col.append(place(cb_[:, 0:1] // TOK, rank_col))

    pick = jnp.zeros((ROWS, TOK), F32)
    for k in range(2):
        a = hot(pos_row[k] - my_first == iota((ROWS, CAP), 0))
        b = hot(ch_col[k] - e * TOK == iota((CAP, TOK), 1))
        pick += dot(a, b)
    pick = pick.astype(BF)

    loads[0].wait()
    loads[1].wait()
    loads[2].start()
    loads[3].start()

    @pl.loop(0, NX)
    def _(i):
        cols = pl.ds(pl.multiple_of(i * BLK, BLK), BLK)
        xr = dot(pick, tok[:, cols]).astype(BF)
        dr = dot(pick, grad[:, cols]).astype(BF)
        for j in range(NY):
            for k in range(2):
                at = slice((2 * j + k) * COL, (2 * j + k + 1) * COL)
                pk[k, i, j, 0] = xr[:, at]
                pk[k, i, j, 1] = dr[:, at]

    pl.semaphore_wait(barrier, PLANE - 1 + NZ - 1)

    def forth(i):
        px, py, pc = partner(i)
        return pltpu.make_async_remote_copy(
            src_ref=pk.at[pc, px, py], dst_ref=rp.at[c, x, y], send_sem=asem.at[i],
            recv_sem=arsem.at[i], device_id=dev(r, px, py, pc), device_id_type=MESH,
        )

    @pl.loop(1, PLANE)
    def _(i):
        forth(i).start()

    rp[c, x, y] = pk[c, x, y]
    gather = jnp.concatenate([hot(pos_col[k] == iota((CAP, PAD), 1)) for k in range(2)], axis=0)
    for k in range(2):
        gate_col.append(jnp.broadcast_to(gates_ref[0, k : k + 1, :], sq).T)
        gc[k * 8 : (k + 1) * 8] = gate_col[k].reshape(8, ROWS, COL)

    @pl.loop(1, PLANE)
    def _(i):
        forth(i).wait_recv()

    both = jnp.concatenate([rp[:, :, :, k].reshape(PAD, COL) for k in range(2)], axis=1)
    both = dot(gather, both).astype(BF)
    for a in range(2):
        for k in range(2):
            xc[a, k, c, x, y] = both[k * CAP : (k + 1) * CAP, a * COL : (a + 1) * COL]

    p1 = [[], []]
    for a in range(2):
        for d in (1, 3, 2):
            for k, to in ((0, dev(r, xs(d), y, c)), (1, dev(r, x, ys(d), c))):
                p1[a].append(send(xc.at[a, k, c, x, y], xc.at[a, k, c, x, y], to))

    def row(a, k, d):
        return xc.at[a, 0, c, :, ys(d)] if k == 0 else xc.at[a, 1, c, xs(d)]

    def half(a, k, d, h):
        return xc.at[a, 0, c, 2 * h : 2 * h + 2, ys(d)] if k == 0 else xc.at[a, 1, c, xs(d), 2 * h : 2 * h + 2]

    def along(k, d):
        return dev(r, x, ys(d), c) if k == 0 else dev(r, xs(d), y, c)

    p2, fw, sibs = [[], []], [[], []], [[], []]
    for a in range(2):
        for cp in p1[a]:
            cp.wait_recv()
        for k in range(2):
            p2[a].append(send(row(a, k, 0), row(a, k, 0), along(k, 1)))
            p2[a].append(send(row(a, k, 0), row(a, k, 0), along(k, 3)))
        for k in range(2):
            sibs[a].append(send(row(a, k, 0), row(a, k, 0), sib))
    loads[2].wait()
    loads[3].wait()
    for a in range(2):
        for k in range(2):
            p2[a][2 * k].wait_recv()
            fw[a].append(send(half(a, k, 3, 0), half(a, k, 3, 0), along(k, 1)))
            p2[a][2 * k + 1].wait_recv()
            fw[a].append(send(half(a, k, 1, 1), half(a, k, 1, 1), along(k, 3)))
        for k in range(2):
            for d in (3, 1):
                sibs[a].append(send(row(a, k, d), row(a, k, d), sib))

    right, left = dev(zs(1), x, y, c), dev(zs(7), x, y, c)
    ring = [None, None]

    def zstep(w, s):
        if s > 1:
            for cp in ring[w]:
                cp.wait_recv()
        if s < 4:
            ra, la = zb.at[w, zs(9 - s)], zb.at[w, zs(s - 1)]
        elif s == 4:
            ra, la = zb.at[w, zs(5), 0], zb.at[w, zs(3), 1]
        else:
            return
        ring[w] = [send(ra, ra, right), send(la, la, left)]

    acc[...] = jnp.zeros_like(acc)
    acts, dhs, backs = [], [], []
    for a in range(2):
        for cp in fw[a]:
            cp.wait_recv()
        for k in range(2):
            sibs[a].append(send(row(a, k, 2), row(a, k, 2), sib))
        for cp in sibs[a]:
            cp.wait_recv()

        @pl.loop(0, NX)
        def _(i):
            cols = pl.ds(pl.multiple_of(i * BLK, BLK), BLK)
            for k in range(2):
                lhs = jnp.concatenate(
                    [xc[a, k, h, i, j] for j in range(NY) for h in range(2)], axis=1
                )
                if a == 0:
                    acc[0, k] += dot(lhs, win[k, cols, :])
                else:
                    acc[1, k] += dot(lhs, wout[k, :, cols], 1, 1)

        if a == 0:
            slopes = []
            for k in range(2):
                hidden = acc[0, k]
                tang = jnp.tanh(GELU_SCALE * (hidden + GELU_CUBIC * hidden * hidden * hidden))
                acts.append((0.5 * hidden * (1.0 + tang)).astype(BF))
                slope = 0.5 * (1.0 + tang) + 0.5 * hidden * (1.0 - tang * tang) * GELU_SCALE * (
                    1.0 + 3.0 * GELU_CUBIC * hidden * hidden
                )
                acc[0, k] = slope
                zb[0, r, k] = acts[k]
            zstep(0, 1)
    for k in range(2):
        dhs.append((gate_col[k][:, 0:1] * acc[1, k] * acc[0, k]).astype(BF))
        zb[1, r, k] = dhs[k]
    zstep(1, 1)
    zstep(0, 2)
    for k in range(2):
        gbuf[0, k] = lax.dot_general(
            jnp.ones((8, F), F32), zb[0, r, k].astype(F32) * acc[1, k], (((1,), (1,)), ((), ())),
            precision=lax.Precision.HIGHEST, preferred_element_type=F32,
        )
    g0 = send(gbuf.at[0], gsib, sib)

    factor = jnp.where(c == 0, 1.0, gc[chip])
    slots = pl.ds(pl.multiple_of(lax.rem(chip, 8) * ROWS, ROWS), ROWS)

    @pl.loop(0, NX)
    def _(i):
        for j in range(NY):
            for h in range(2):
                eb[i, j, h] = (factor * xc[c, x // 2, h, i, j, slots, :].astype(F32)).astype(BF)

    ex = []
    for d in (1, 7, 2, 6, 3, 5, 4):
        to = zs(d)
        ex.append(send(eb.at[to // 2, pl.ds(2 * lax.rem(to, 2), 2)], ds.at[c, x, y, r], dev(to, x, y, c)))
    ds[c, x, y, r] = eb[r // 2, pl.ds(2 * lax.rem(r, 2), 2)]

    pair = []
    for k in range(2):

        @pl.loop(0, NX)
        def _(i):
            cols = pl.ds(pl.multiple_of(i * BLK, BLK), BLK)
            part = dot(zb[1, r, k], win[k, cols, :], 1, 1).astype(BF)
            for j in range(NY):
                for h in range(2):
                    ps[k, h, i, j] = part[:, (2 * j + h) * COL : (2 * j + h + 1) * COL]

        pair.append(send(ps.at[k, oc], rsib.at[k], sib))

    for cp in ex:
        cp.wait_recv()
    q1 = []
    for d in (1, 3, 2):
        q1.append(send(ds.at[c, x, y, 0:4], ds.at[c, x, y, 0:4], dev(r, xs(d), y, c)))
        q1.append(send(ds.at[c, x, y, 4:8], ds.at[c, x, y, 4:8], dev(r, x, ys(d), c)))

    zstep(1, 2)

    stage1 = [[], []]
    for k in range(2):
        pair[k].wait_recv()

        @pl.loop(0, NX)
        def _(i):
            for j in range(NY):
                ps[k, c, i, j] = (ps[k, c, i, j].astype(F32) + rsib[k, i, j].astype(F32)).astype(BF)

        for d in (1, 3, 2):
            if k == 0:
                stage1[k].append(send(ps.at[0, c, xs(d)], rs1.at[0, x], dev(r, xs(d), y, c)))
            else:
                stage1[k].append(send(ps.at[1, c, :, ys(d)], rs1.at[1, y], dev(r, x, ys(d), c)))

    zstep(0, 3)

    g0.wait_recv()
    gbuf[1] = gbuf[0] + gsib[...]
    gx[x] = gbuf[1]
    g1 = [send(gbuf.at[1], gx.at[x], dev(r, xs(d), y, c)) for d in (1, 3, 2)]

    for cp in q1:
        cp.wait_recv()
    q2 = []
    for d in (1, 3, 2):
        q2.append(send(ds.at[c, :, y, 0:4], ds.at[c, :, y, 0:4], dev(r, x, ys(d), c)))
        q2.append(send(ds.at[c, x, :, 4:8], ds.at[c, x, :, 4:8], dev(r, xs(d), y, c)))
    zstep(1, 3)

    stage2 = [[], []]
    for k in range(2):
        for cp in stage1[k]:
            cp.wait_recv()
        for j in range(4):
            total = (ps[0, c, x, j] if k == 0 else ps[1, c, j, y]).astype(F32)
            for d in (1, 2, 3):
                total += rs1[k, xs(d) if k == 0 else ys(d), j].astype(F32)
            ts[k, j] = total.astype(BF)
        for d in (1, 3, 2):
            if k == 0:
                stage2[k].append(send(ts.at[0, ys(d)], rs2.at[0, y], dev(r, x, ys(d), c)))
            else:
                stage2[k].append(send(ts.at[1, xs(d)], rs2.at[1, x], dev(r, xs(d), y, c)))

    zstep(0, 4)
    for cp in g1:
        cp.wait_recv()
    gbuf[2] = (gx[0] + gx[1]) + (gx[2] + gx[3])
    gy[y] = gbuf[2]
    g2 = [send(gbuf.at[2], gy.at[y], dev(r, x, ys(d), c)) for d in (1, 3, 2)]

    expand = jnp.concatenate([hot(pos_row[k] == iota((PAD, CAP), 0)) for k in range(2)], axis=1)
    sums = []
    for k in range(2):
        for cp in stage2[k]:
            cp.wait_recv()
        total = ts[k, y if k == 0 else x].astype(F32)
        for d in (1, 2, 3):
            total += rs2[k, ys(d) if k == 0 else xs(d)].astype(F32)
        sums.append(total.astype(BF))
    ob[...] = dot(expand, jnp.concatenate(sums, axis=0)).astype(BF).reshape(2, NX, NY, ROWS, COL)

    def back(i):
        px, py, pc = partner(i)
        return pltpu.make_async_remote_copy(
            src_ref=ob.at[pc, px, py], dst_ref=rb.at[c, x, y], send_sem=bsem.at[i],
            recv_sem=brsem.at[i], device_id=dev(r, px, py, pc), device_id_type=MESH,
        )

    @pl.loop(1, PLANE)
    def _(i):
        back(i).start()

    rb[c, x, y] = ob[c, x, y]
    zstep(1, 4)

    for cp in q2:
        cp.wait_recv()
    q3 = send(ds.at[c], ds.at[c], sib)

    unpick = jnp.zeros((TOK, ROWS), F32)
    for k in range(2):
        bt = hot(ch_row[k] - e * TOK == iota((TOK, CAP), 0))
        at = hot(pos_col[k] - my_first == iota((CAP, ROWS), 1))
        unpick += dot(bt, at)
    unpick_ref[...] = unpick.astype(BF)

    for cp in g2:
        cp.wait_recv()
    total = (gy[0] + gy[1]) + (gy[2] + gy[3])
    for k in range(2):
        dgate_ref[0, k : k + 1, :] = total[k, 0:1, :]

    zstep(0, 5)
    zstep(1, 5)
    q3.wait_recv()
    for k in range(2):
        act = zb[0, :, k].reshape(NZ * CAP, F)
        dh = zb[1, :, k].reshape(NZ * CAP, F)

        def cols(a, j, h):
            return jnp.concatenate(
                [ds[a, 2 * k : 2 * k + 2, :, g, j, h].reshape(CAP, COL) for g in range(NZ)], axis=0
            )

        for j in range(2):
            xk = jnp.concatenate([cols(0, j, h) for h in range(2)], axis=1)
            sk = jnp.concatenate([cols(1, j, h) for h in range(2)], axis=1)
            dwin_ref[k, j * 256 : (j + 1) * 256, :] = dot(xk, dh, 0, 0).astype(BF)
            dwout_ref[k, :, j * 256 : (j + 1) * 256] = dot(act, sk, 0, 0).astype(BF)

    @pl.loop(1, PLANE)
    def _(i):
        back(i).wait_recv()

    rows_ref[...] = rb[...]

    assert counter[0] <= NSEM, counter[0]
    for cp in sent:
        cp.wait_send()

    @pl.loop(1, PLANE)
    def _(i):
        forth(i).wait_send()
        back(i).wait_send()


def finish(rows_ref, unpick_ref, gate_ref, win_ref, wout_ref, dtok_ref, dgate_ref, dwin_ref, dwout_ref, sem):
    copies = [
        pltpu.make_async_copy(win_ref, dwin_ref, sem.at[0]),
        pltpu.make_async_copy(wout_ref, dwout_ref, sem.at[1]),
    ]
    for cp in copies:
        cp.start()
    dgate_ref[...] = gate_ref[...]
    for i in range(NX):
        rows = jnp.concatenate([rows_ref[h, i, j] for j in range(NY) for h in range(2)], axis=1)
        dtok_ref[0, :, i * BLK : (i + 1) * BLK] = dot(unpick_ref[...], rows).astype(BF)
    for cp in copies:
        cp.wait()


def local(tokens, grad_out, gates, chosen, w_in, w_out):
    hbm = pl.BlockSpec(memory_space=pl.ANY)
    vmem = pl.BlockSpec(memory_space=pltpu.VMEM)
    dma = pltpu.SemaphoreType.DMA
    d_gate = jax.ShapeDtypeStruct((1, 2, CAP), F32)
    d_in = jax.ShapeDtypeStruct((2, D // NZ, F), BF)
    d_out = jax.ShapeDtypeStruct((2, F, D // NZ), BF)
    parts = pl.pallas_call(
        kernel,
        out_shape=(
            jax.ShapeDtypeStruct((2, NX, NY, ROWS, COL), BF),
            jax.ShapeDtypeStruct((TOK, ROWS), BF),
            d_gate,
            d_in,
            d_out,
        ),
        in_specs=[hbm, hbm, vmem, vmem, hbm, hbm],
        out_specs=(vmem,) * 5,
        scratch_shapes=[
            pltpu.VMEM((TOK, D), BF),
            pltpu.VMEM((TOK, D), BF),
            pltpu.VMEM((2, D, F), BF),
            pltpu.VMEM((2, F, D), BF),
            pltpu.VMEM((2, NX, NY, 2, ROWS, COL), BF),
            pltpu.VMEM((2, NX, NY, 2, ROWS, COL), BF),
            pltpu.VMEM((2, 2, 2, NX, NY, CAP, COL), BF),
            pltpu.VMEM((NX * NY, ROWS, COL), F32),
            pltpu.VMEM((NX, NY, 2, ROWS, COL), BF),
            pltpu.VMEM((2, NX, NY, NZ, 2, 2, ROWS, COL), BF),
            pltpu.VMEM((2, NZ, 2, CAP, F), BF),
            pltpu.VMEM((2, 2, CAP, F), F32),
            pltpu.VMEM((2, 2, NX, NY, CAP, COL), BF),
            pltpu.VMEM((2, NX, NY, CAP, COL), BF),
            pltpu.VMEM((2, 4, 4, CAP, COL), BF),
            pltpu.VMEM((2, 4, CAP, COL), BF),
            pltpu.VMEM((2, 4, CAP, COL), BF),
            pltpu.VMEM((2, NX, NY, ROWS, COL), BF),
            pltpu.VMEM((2, NX, NY, ROWS, COL), BF),
            pltpu.VMEM((3, 2, 8, CAP), F32),
            pltpu.VMEM((2, 8, CAP), F32),
            pltpu.VMEM((4, 2, 8, CAP), F32),
            pltpu.VMEM((4, 2, 8, CAP), F32),
            dma((NSEM,)),
            dma((NSEM,)),
            dma((PLANE,)),
            dma((PLANE,)),
            dma((PLANE,)),
            dma((PLANE,)),
            dma((4,)),
        ],
        compiler_params=pltpu.CompilerParams(
            collective_id=0, has_side_effects=True, vmem_limit_bytes=60 << 20
        ),
        name="expert_backward",
    )(tokens, grad_out, gates, chosen, w_in, w_out)
    return pl.pallas_call(
        finish,
        out_shape=(jax.ShapeDtypeStruct((1, TOK, D), BF), d_gate, d_in, d_out),
        in_specs=[vmem, vmem, vmem, hbm, hbm],
        out_specs=(vmem, vmem, hbm, hbm),
        scratch_shapes=[dma((2,))],
        compiler_params=pltpu.CompilerParams(vmem_limit_bytes=60 << 20),
        name="finish",
    )(*parts)


def solution(mesh):
    return jax.shard_map(
        local,
        mesh=mesh,
        in_specs=(
            P("rep", "exp", None),
            P("rep", "exp", None),
            P("rep", None, None),
            P("rep", None, None),
            P(None, None, "exp"),
            P(None, "exp", None),
        ),
        out_specs=(
            P("rep", "exp", None),
            P("rep", None, None),
            P(None, "rep", "exp"),
            P(None, "exp", "rep"),
        ),
        check_vma=False,
    )
```

time: 102 us -> 120 us (1.18)
  Pallas kernels: 93.9 us -> 119 us
  local copies, waits for them, and re-layouts: 7.25 us -> 0 us
    pallas_call x1 -> x2, Pallas kernels: 93.9 us -> 119 us  [the longest x1 84.4 us: local(): pl.pallas_call(kernel, out_shape=(jax.ShapeDtypeStruct((2, NX, NY, ROWS,...]
    unnamed x4 -> x0, local copies, waits for them, and re-layouts: 7.25 us -> none
where the time goes in v2:
time: 120 us
  Pallas kernels  119 us (99%)
    pallas_call x1, Pallas kernels, local(): pl.pallas_call(kernel, out_shape=(jax.ShapeDtypeStruct((2, NX, NY, ROWS,...  84.4 us
    pallas_call x1, Pallas kernels, local(): pl.pallas_call(finish, out_shape=(jax.ShapeDtypeStruct((1, TOK, D), BF),...  34.8 us

profile of v2, /device:TPU:1, one launch (start us, length us, event | category | flops | bytes accessed | tf_op | source)
XLA Modules:
  0.0 119.8 jit_solution(15920045370990992376)
XLA Ops:
  0.6 84.4 %expert_backward.1 = (bf16[2,4,4,16,128]{4,3,2,1,0:T(8,128)(2,1)}, bf16[128,16]{1,0:T(8,128)(2,1)}, f32[1,2,128]{2,1,0:T(2,128)}, bf16[2,512,256]{2,1,0:T(8,128)(2,1)}, bf16[2,256,512]{2,1,0:T(8,128)(2,1)}) custom-call(bf16[1,128,4096]{2,1,0:T(8,128)(2,1)} %tok_hbm.1, bf16[1,128,4096]{2,1,0:T(8,128)(2,1)} %grad_hbm.1, f32[1,2,128]{2,1,0:T(2,128)} %gates_ref.1, ...), custom_call_target="tpu_custom_call" | custom-call | tf_op jit(solution)/shard_map/expert_backward/pallas_call | solution.py:460
  85.0 34.8 %finish.1 = (bf16[1,128,4096]{2,1,0:T(8,128)(2,1)}, f32[1,2,128]{2,1,0:T(2,128)}, bf16[2,512,256]{2,1,0:T(8,128)(2,1)}, bf16[2,256,512]{2,1,0:T(8,128)(2,1)}) custom-call(bf16[2,4,4,16,128]{4,3,2,1,0:T(8,128)(2,1)} %get-tuple-element.9.rows_ref, bf16[128,16]{1,0:T(8,128)(2,1)} %get-tuple-element.10.unpick_ref, f32[1,2,128]{2,1,0:T(2,128)} %get-tuple-element.11.gate_ref, ...), custom_call_target="tpu_custom_call" | custom-call | tf_op jit(solution)/shard_map/finish/pallas_call | solution.py:508

commit v3 on v2

--- a/solution.py
+++ b/solution.py
@@ -24,7 +24,7 @@
 BLK = D // NX
 PLANE = NX * NY * 2
 
-NSEM = 104
+NSEM = 144
 
 
 def dot(a, b, ca=1, cb=0):
@@ -69,16 +69,11 @@
     loads[0].start()
     loads[1].start()
 
-    def partner(i):
-        return lax.rem(x + i // 8, 4), lax.rem(y + (i // 2) % 4, 4), lax.rem(c + i, 2)
-
     barrier = pltpu.get_barrier_semaphore()
 
-    @pl.loop(1, PLANE)
-    def _(i):
-        px, py, pc = partner(i)
-        pl.semaphore_signal(barrier, inc=1, device_id=dev(r, px, py, pc), device_id_type=MESH)
-
+    for i in range(1, PLANE):
+        to = dev(r, xs(i // 8), ys((i // 2) % 4), oc if i % 2 else c)
+        pl.semaphore_signal(barrier, inc=1, device_id=to, device_id_type=MESH)
     for d in range(1, NZ):
         pl.semaphore_signal(barrier, inc=1, device_id=dev(zs(d), x, y, c), device_id_type=MESH)
 
@@ -146,26 +141,27 @@
 
     pl.semaphore_wait(barrier, PLANE - 1 + NZ - 1)
 
-    def forth(i):
-        px, py, pc = partner(i)
-        return pltpu.make_async_remote_copy(
-            src_ref=pk.at[pc, px, py], dst_ref=rp.at[c, x, y], send_sem=asem.at[i],
-            recv_sem=arsem.at[i], device_id=dev(r, px, py, pc), device_id_type=MESH,
-        )
-
-    @pl.loop(1, PLANE)
-    def _(i):
-        forth(i).start()
-
+    def plane(src, dst, s_sem, r_sem):
+        copies = []
+        for i in range(1, PLANE):
+            px, py, pc = xs(i // 8), ys((i // 2) % 4), (oc if i % 2 else c)
+            cp = pltpu.make_async_remote_copy(
+                src_ref=src.at[pc, px, py], dst_ref=dst.at[c, x, y], send_sem=s_sem.at[i],
+                recv_sem=r_sem.at[i], device_id=dev(r, px, py, pc), device_id_type=MESH,
+            )
+            cp.start()
+            copies.append(cp)
+        return copies
+
+    forth = plane(pk, rp, asem, arsem)
     rp[c, x, y] = pk[c, x, y]
     gather = jnp.concatenate([hot(pos_col[k] == iota((CAP, PAD), 1)) for k in range(2)], axis=0)
     for k in range(2):
         gate_col.append(jnp.broadcast_to(gates_ref[0, k : k + 1, :], sq).T)
         gc[k * 8 : (k + 1) * 8] = gate_col[k].reshape(8, ROWS, COL)
 
-    @pl.loop(1, PLANE)
-    def _(i):
-        forth(i).wait_recv()
+    for cp in forth:
+        cp.wait_recv()
 
     both = jnp.concatenate([rp[:, :, :, k].reshape(PAD, COL) for k in range(2)], axis=1)
     both = dot(gather, both).astype(BF)
@@ -173,41 +169,83 @@
         for k in range(2):
             xc[a, k, c, x, y] = both[k * CAP : (k + 1) * CAP, a * COL : (a + 1) * COL]
 
-    p1 = [[], []]
-    for a in range(2):
-        for d in (1, 3, 2):
-            for k, to in ((0, dev(r, xs(d), y, c)), (1, dev(r, x, ys(d), c))):
-                p1[a].append(send(xc.at[a, k, c, x, y], xc.at[a, k, c, x, y], to))
-
-    def row(a, k, d):
-        return xc.at[a, 0, c, :, ys(d)] if k == 0 else xc.at[a, 1, c, xs(d)]
-
-    def half(a, k, d, h):
-        return xc.at[a, 0, c, 2 * h : 2 * h + 2, ys(d)] if k == 0 else xc.at[a, 1, c, xs(d), 2 * h : 2 * h + 2]
-
-    def along(k, d):
-        return dev(r, x, ys(d), c) if k == 0 else dev(r, xs(d), y, c)
-
-    p2, fw, sibs = [[], []], [[], []], [[], []]
-    for a in range(2):
-        for cp in p1[a]:
-            cp.wait_recv()
-        for k in range(2):
-            p2[a].append(send(row(a, k, 0), row(a, k, 0), along(k, 1)))
-            p2[a].append(send(row(a, k, 0), row(a, k, 0), along(k, 3)))
-        for k in range(2):
-            sibs[a].append(send(row(a, k, 0), row(a, k, 0), sib))
+    class Spread:
+        def __init__(self, row):
+            self.row = row
+
+        def block(self, k):
+            return self.row(k, 0, x if k == 0 else y)
+
+        def first(self):
+            self.got = []
+            for d in (1, 3, 2):
+                for k, to in ((0, dev(r, xs(d), y, c)), (1, dev(r, x, ys(d), c))):
+                    ref = self.block(k)
+                    self.got.append(send(ref, ref, to))
+
+        def along(self, k, d):
+            return dev(r, x, ys(d), c) if k == 0 else dev(r, xs(d), y, c)
+
+        def second(self):
+            for cp in self.got:
+                cp.wait_recv()
+            self.got = []
+            for k in range(2):
+                ref = self.row(k, 0, slice(0, 4))
+                for d in (1, 3):
+                    self.got.append(send(ref, ref, self.along(k, d)))
+            self.sibs = [send(self.row(k, 0, slice(0, 4)), self.row(k, 0, slice(0, 4)), sib) for k in range(2)]
+
+        def forward(self):
+            got, self.got = self.got, []
+            for k in range(2):
+                for n, (d, at) in enumerate(((3, slice(0, 2)), (1, slice(2, 4)))):
+                    got[2 * k + n].wait_recv()
+                    ref = self.row(k, d, at)
+                    self.got.append(send(ref, ref, self.along(k, 1 if d == 3 else 3)))
+            for k in range(2):
+                for d in (3, 1):
+                    ref = self.row(k, d, slice(0, 4))
+                    self.sibs.append(send(ref, ref, sib))
+
+        def last(self):
+            for cp in self.got:
+                cp.wait_recv()
+            for k in range(2):
+                ref = self.row(k, 2, slice(0, 4))
+                self.sibs.append(send(ref, ref, sib))
+
+        def done(self):
+            for cp in self.sibs:
+                cp.wait_recv()
+
+    def rows_of(a):
+        return lambda k, d, at: xc.at[a, 0, c, at, ys(d)] if k == 0 else xc.at[a, 1, c, xs(d), at]
+
+    def columns_of(a):
+        return lambda k, d, at: ds.at[a, c, at, ys(d), 0:4] if k == 0 else ds.at[a, c, xs(d), at, 4:8]
+
+    own_rows = [Spread(rows_of(a)) for a in range(2)]
+    all_rows = [Spread(columns_of(a)) for a in range(2)]
+    for sp in own_rows:
+        sp.first()
+    for sp in own_rows:
+        sp.second()
     loads[2].wait()
     loads[3].wait()
-    for a in range(2):
-        for k in range(2):
-            p2[a][2 * k].wait_recv()
-            fw[a].append(send(half(a, k, 3, 0), half(a, k, 3, 0), along(k, 1)))
-            p2[a][2 * k + 1].wait_recv()
-            fw[a].append(send(half(a, k, 1, 1), half(a, k, 1, 1), along(k, 3)))
-        for k in range(2):
-            for d in (3, 1):
-                sibs[a].append(send(row(a, k, d), row(a, k, d), sib))
+    for sp in own_rows:
+        sp.forward()
+
+    slots = pl.ds(pl.multiple_of(lax.rem(chip, 8) * ROWS, ROWS), ROWS)
+
+    def two(to):
+        return pl.ds(2 * lax.rem(to, 2), 2)
+
+    def exchange(a, src):
+        copies = []
+        for d in (1, 7, 2, 6, 3, 5, 4):
+            copies.append(send(src(zs(d)), ds.at[a, c, x, y, r], dev(zs(d), x, y, c)))
+        return copies
 
     right, left = dev(zs(1), x, y, c), dev(zs(7), x, y, c)
     ring = [None, None]
@@ -225,14 +263,13 @@
         ring[w] = [send(ra, ra, right), send(la, la, left)]
 
     acc[...] = jnp.zeros_like(acc)
-    acts, dhs, backs = [], [], []
+    acts, dhs = [], []
     for a in range(2):
-        for cp in fw[a]:
-            cp.wait_recv()
-        for k in range(2):
-            sibs[a].append(send(row(a, k, 2), row(a, k, 2), sib))
-        for cp in sibs[a]:
-            cp.wait_recv()
+        own_rows[a].last()
+        if a == 0:
+            ex0 = exchange(0, lambda to: xc.at[0, x // 2, c, to // 2, two(to), slots])
+            ds[0, c, x, y, r] = xc[0, x // 2, c, r // 2, two(r), slots, :]
+        own_rows[a].done()
 
         @pl.loop(0, NX)
         def _(i):
@@ -247,7 +284,6 @@
                     acc[1, k] += dot(lhs, wout[k, :, cols], 1, 1)
 
         if a == 0:
-            slopes = []
             for k in range(2):
                 hidden = acc[0, k]
                 tang = jnp.tanh(GELU_SCALE * (hidden + GELU_CUBIC * hidden * hidden * hidden))
@@ -258,6 +294,9 @@
                 acc[0, k] = slope
                 zb[0, r, k] = acts[k]
             zstep(0, 1)
+            for cp in ex0:
+                cp.wait_recv()
+            all_rows[0].first()
     for k in range(2):
         dhs.append((gate_col[k][:, 0:1] * acc[1, k] * acc[0, k]).astype(BF))
         zb[1, r, k] = dhs[k]
@@ -270,20 +309,14 @@
         )
     g0 = send(gbuf.at[0], gsib, sib)
 
-    factor = jnp.where(c == 0, 1.0, gc[chip])
-    slots = pl.ds(pl.multiple_of(lax.rem(chip, 8) * ROWS, ROWS), ROWS)
 
     @pl.loop(0, NX)
     def _(i):
         for j in range(NY):
-            for h in range(2):
-                eb[i, j, h] = (factor * xc[c, x // 2, h, i, j, slots, :].astype(F32)).astype(BF)
-
-    ex = []
-    for d in (1, 7, 2, 6, 3, 5, 4):
-        to = zs(d)
-        ex.append(send(eb.at[to // 2, pl.ds(2 * lax.rem(to, 2), 2)], ds.at[c, x, y, r], dev(to, x, y, c)))
-    ds[c, x, y, r] = eb[r // 2, pl.ds(2 * lax.rem(r, 2), 2)]
+            eb[i, j] = (gc[chip] * xc[1, x // 2, c, i, j, slots, :].astype(F32)).astype(BF)
+
+    ex1 = exchange(1, lambda to: eb.at[to // 2, two(to)])
+    ds[1, c, x, y, r] = eb[r // 2, two(r)]
 
     pair = []
     for k in range(2):
@@ -297,14 +330,10 @@
                     ps[k, h, i, j] = part[:, (2 * j + h) * COL : (2 * j + h + 1) * COL]
 
         pair.append(send(ps.at[k, oc], rsib.at[k], sib))
-
-    for cp in ex:
-        cp.wait_recv()
-    q1 = []
-    for d in (1, 3, 2):
-        q1.append(send(ds.at[c, x, y, 0:4], ds.at[c, x, y, 0:4], dev(r, xs(d), y, c)))
-        q1.append(send(ds.at[c, x, y, 4:8], ds.at[c, x, y, 4:8], dev(r, x, ys(d), c)))
-
+        if k == 0:
+            all_rows[0].second()
+
+    all_rows[0].forward()
     zstep(1, 2)
 
     stage1 = [[], []]
@@ -329,12 +358,10 @@
     gx[x] = gbuf[1]
     g1 = [send(gbuf.at[1], gx.at[x], dev(r, xs(d), y, c)) for d in (1, 3, 2)]
 
-    for cp in q1:
+    for cp in ex1:
         cp.wait_recv()
-    q2 = []
-    for d in (1, 3, 2):
-        q2.append(send(ds.at[c, :, y, 0:4], ds.at[c, :, y, 0:4], dev(r, x, ys(d), c)))
-        q2.append(send(ds.at[c, x, :, 4:8], ds.at[c, x, :, 4:8], dev(r, xs(d), y, c)))
+    all_rows[1].first()
+    all_rows[0].last()
     zstep(1, 3)
 
     stage2 = [[], []]
@@ -352,6 +379,7 @@
             else:
                 stage2[k].append(send(ts.at[1, xs(d)], rs2.at[1, x], dev(r, xs(d), y, c)))
 
+    all_rows[1].second()
     zstep(0, 4)
     for cp in g1:
         cp.wait_recv()
@@ -370,23 +398,11 @@
         sums.append(total.astype(BF))
     ob[...] = dot(expand, jnp.concatenate(sums, axis=0)).astype(BF).reshape(2, NX, NY, ROWS, COL)
 
-    def back(i):
-        px, py, pc = partner(i)
-        return pltpu.make_async_remote_copy(
-            src_ref=ob.at[pc, px, py], dst_ref=rb.at[c, x, y], send_sem=bsem.at[i],
-            recv_sem=brsem.at[i], device_id=dev(r, px, py, pc), device_id_type=MESH,
-        )
-
-    @pl.loop(1, PLANE)
-    def _(i):
-        back(i).start()
-
+    back = plane(ob, rb, bsem, brsem)
     rb[c, x, y] = ob[c, x, y]
     zstep(1, 4)
 
-    for cp in q2:
-        cp.wait_recv()
-    q3 = send(ds.at[c], ds.at[c], sib)
+    all_rows[1].forward()
 
     unpick = jnp.zeros((TOK, ROWS), F32)
     for k in range(2):
@@ -401,16 +417,18 @@
     for k in range(2):
         dgate_ref[0, k : k + 1, :] = total[k, 0:1, :]
 
+    all_rows[1].last()
     zstep(0, 5)
     zstep(1, 5)
-    q3.wait_recv()
+    for sp in all_rows:
+        sp.done()
     for k in range(2):
         act = zb[0, :, k].reshape(NZ * CAP, F)
         dh = zb[1, :, k].reshape(NZ * CAP, F)
 
         def cols(a, j, h):
             return jnp.concatenate(
-                [ds[a, 2 * k : 2 * k + 2, :, g, j, h].reshape(CAP, COL) for g in range(NZ)], axis=0
+                [ds[a, h, 2 * k : 2 * k + 2, :, g, j].reshape(CAP, COL) for g in range(NZ)], axis=0
             )
 
         for j in range(2):
@@ -419,35 +437,25 @@
             dwin_ref[k, j * 256 : (j + 1) * 256, :] = dot(xk, dh, 0, 0).astype(BF)
             dwout_ref[k, :, j * 256 : (j + 1) * 256] = dot(act, sk, 0, 0).astype(BF)
 
-    @pl.loop(1, PLANE)
-    def _(i):
-        back(i).wait_recv()
-
+    for cp in back:
+        cp.wait_recv()
     rows_ref[...] = rb[...]
 
     assert counter[0] <= NSEM, counter[0]
     for cp in sent:
         cp.wait_send()
 
-    @pl.loop(1, PLANE)
-    def _(i):
-        forth(i).wait_send()
-        back(i).wait_send()
-
-
-def finish(rows_ref, unpick_ref, gate_ref, win_ref, wout_ref, dtok_ref, dgate_ref, dwin_ref, dwout_ref, sem):
-    copies = [
-        pltpu.make_async_copy(win_ref, dwin_ref, sem.at[0]),
-        pltpu.make_async_copy(wout_ref, dwout_ref, sem.at[1]),
-    ]
-    for cp in copies:
-        cp.start()
-    dgate_ref[...] = gate_ref[...]
+    for cp in forth + back:
+        cp.wait_send()
+
+
+def finish(rows_ref, unpick_ref, gate_ref, win_ref, wout_ref, dtok_ref, dgate_ref, dwin_ref, dwout_ref):
     for i in range(NX):
         rows = jnp.concatenate([rows_ref[h, i, j] for j in range(NY) for h in range(2)], axis=1)
         dtok_ref[0, :, i * BLK : (i + 1) * BLK] = dot(unpick_ref[...], rows).astype(BF)
-    for cp in copies:
-        cp.wait()
+    dgate_ref[...] = gate_ref[...]
+    dwin_ref[...] = win_ref[...]
+    dwout_ref[...] = wout_ref[...]
 
 
 def local(tokens, grad_out, gates, chosen, w_in, w_out):
@@ -477,8 +485,8 @@
             pltpu.VMEM((2, NX, NY, 2, ROWS, COL), BF),
             pltpu.VMEM((2, 2, 2, NX, NY, CAP, COL), BF),
             pltpu.VMEM((NX * NY, ROWS, COL), F32),
-            pltpu.VMEM((NX, NY, 2, ROWS, COL), BF),
-            pltpu.VMEM((2, NX, NY, NZ, 2, 2, ROWS, COL), BF),
+            pltpu.VMEM((NX, NY, ROWS, COL), BF),
+            pltpu.VMEM((2, 2, NX, NY, NZ, 2, ROWS, COL), BF),
             pltpu.VMEM((2, NZ, 2, CAP, F), BF),
             pltpu.VMEM((2, 2, CAP, F), F32),
             pltpu.VMEM((2, 2, NX, NY, CAP, COL), BF),
@@ -508,9 +516,8 @@
     return pl.pallas_call(
         finish,
         out_shape=(jax.ShapeDtypeStruct((1, TOK, D), BF), d_gate, d_in, d_out),
-        in_specs=[vmem, vmem, vmem, hbm, hbm],
-        out_specs=(vmem, vmem, hbm, hbm),
-        scratch_shapes=[dma((2,))],
+        in_specs=[vmem] * 5,
+        out_specs=(vmem,) * 4,
         compiler_params=pltpu.CompilerParams(vmem_limit_bytes=60 << 20),
         name="finish",
     )(*parts)

time: 120 us -> 81.3 us (0.68)
  Pallas kernels: 119 us -> 80.5 us
    pallas_call x1, Pallas kernels: 34.8 us -> 2.94 us  [local(): pl.pallas_call(finish, out_shape=(jax.ShapeDtypeStruct((1, TOK, D), BF),...]
    pallas_call x1, Pallas kernels: 84.4 us -> 77.6 us  [local(): pl.pallas_call(kernel, out_shape=(jax.ShapeDtypeStruct((2, NX, NY, ROWS,...]
where the time goes in v3:
time: 81.3 us; the launch traced here: 81.2 us
  Pallas kernels  80.5 us (99%)
    pallas_call x1, Pallas kernels, local(): pl.pallas_call(kernel, out_shape=(jax.ShapeDtypeStruct((2, NX, NY, ROWS,...  77.6 us
    pallas_call x1, Pallas kernels, local(): pl.pallas_call(finish, out_shape=(jax.ShapeDtypeStruct((1, TOK, D), BF),...  2.94 us

profile of v3, /device:TPU:1, one launch (start us, length us, event | category | flops | bytes accessed | tf_op | source)
XLA Modules:
  0.0 81.2 jit_solution(4788228411936567983)
XLA Ops:
  0.6 77.6 %expert_backward.1 = (bf16[2,4,4,16,128]{4,3,2,1,0:T(8,128)(2,1)}, bf16[128,16]{1,0:T(8,128)(2,1)}, f32[1,2,128]{2,1,0:T(2,128)}, bf16[2,512,256]{2,1,0:T(8,128)(2,1)}, bf16[2,256,512]{2,1,0:T(8,128)(2,1)}) custom-call(bf16[1,128,4096]{2,1,0:T(8,128)(2,1)} %tok_hbm.1, bf16[1,128,4096]{2,1,0:T(8,128)(2,1)} %grad_hbm.1, f32[1,2,128]{2,1,0:T(2,128)} %gates_ref.1, ...), custom_call_target="tpu_custom_call" | custom-call | tf_op jit(solution)/shard_map/expert_backward/pallas_call | solution.py:468
  78.2 2.9 %finish.1 = (bf16[1,128,4096]{2,1,0:T(8,128)(2,1)}, f32[1,2,128]{2,1,0:T(2,128)}, bf16[2,512,256]{2,1,0:T(8,128)(2,1)}, bf16[2,256,512]{2,1,0:T(8,128)(2,1)}) custom-call(bf16[2,4,4,16,128]{4,3,2,1,0:T(8,128)(2,1)} %get-tuple-element.9.rows_ref, bf16[128,16]{1,0:T(8,128)(2,1)} %get-tuple-element.10.unpick_ref, f32[1,2,128]{2,1,0:T(2,128)} %get-tuple-element.11.gate_ref, ...), custom_call_target="tpu_custom_call" | custom-call | tf_op jit(solution)/shard_map/finish/pallas_call | solution.py:516

commit v4 on v3

--- a/solution.py
+++ b/solution.py
@@ -194,7 +194,8 @@
                 ref = self.row(k, 0, slice(0, 4))
                 for d in (1, 3):
                     self.got.append(send(ref, ref, self.along(k, d)))
-            self.sibs = [send(self.row(k, 0, slice(0, 4)), self.row(k, 0, slice(0, 4)), sib) for k in range(2)]
+            self.sibs = {}
+            self.share(0)
 
         def forward(self):
             got, self.got = self.got, []
@@ -203,21 +204,22 @@
                     got[2 * k + n].wait_recv()
                     ref = self.row(k, d, at)
                     self.got.append(send(ref, ref, self.along(k, 1 if d == 3 else 3)))
-            for k in range(2):
-                for d in (3, 1):
-                    ref = self.row(k, d, slice(0, 4))
-                    self.sibs.append(send(ref, ref, sib))
+            self.share(3)
+            self.share(1)
+
+        def share(self, d):
+            refs = [self.row(k, d, slice(0, 4)) for k in range(2)]
+            self.sibs[d] = [send(ref, ref, sib) for ref in refs]
 
         def last(self):
             for cp in self.got:
                 cp.wait_recv()
-            for k in range(2):
-                ref = self.row(k, 2, slice(0, 4))
-                self.sibs.append(send(ref, ref, sib))
-
-        def done(self):
-            for cp in self.sibs:
-                cp.wait_recv()
+            self.share(2)
+
+        def done(self, rows=(0, 3, 1, 2)):
+            for d in rows:
+                for cp in self.sibs[d]:
+                    cp.wait_recv()
 
     def rows_of(a):
         return lambda k, d, at: xc.at[a, 0, c, at, ys(d)] if k == 0 else xc.at[a, 1, c, xs(d), at]
@@ -227,15 +229,6 @@
 
     own_rows = [Spread(rows_of(a)) for a in range(2)]
     all_rows = [Spread(columns_of(a)) for a in range(2)]
-    for sp in own_rows:
-        sp.first()
-    for sp in own_rows:
-        sp.second()
-    loads[2].wait()
-    loads[3].wait()
-    for sp in own_rows:
-        sp.forward()
-
     slots = pl.ds(pl.multiple_of(lax.rem(chip, 8) * ROWS, ROWS), ROWS)
 
     def two(to):
@@ -262,53 +255,35 @@
             return
         ring[w] = [send(ra, ra, right), send(la, la, left)]
 
-    acc[...] = jnp.zeros_like(acc)
-    acts, dhs = [], []
-    for a in range(2):
-        own_rows[a].last()
-        if a == 0:
-            ex0 = exchange(0, lambda to: xc.at[0, x // 2, c, to // 2, two(to), slots])
-            ds[0, c, x, y, r] = xc[0, x // 2, c, r // 2, two(r), slots, :]
-        own_rows[a].done()
-
-        @pl.loop(0, NX)
-        def _(i):
-            cols = pl.ds(pl.multiple_of(i * BLK, BLK), BLK)
-            for k in range(2):
-                lhs = jnp.concatenate(
-                    [xc[a, k, h, i, j] for j in range(NY) for h in range(2)], axis=1
-                )
-                if a == 0:
-                    acc[0, k] += dot(lhs, win[k, cols, :])
-                else:
-                    acc[1, k] += dot(lhs, wout[k, :, cols], 1, 1)
-
-        if a == 0:
-            for k in range(2):
-                hidden = acc[0, k]
-                tang = jnp.tanh(GELU_SCALE * (hidden + GELU_CUBIC * hidden * hidden * hidden))
-                acts.append((0.5 * hidden * (1.0 + tang)).astype(BF))
-                slope = 0.5 * (1.0 + tang) + 0.5 * hidden * (1.0 - tang * tang) * GELU_SCALE * (
-                    1.0 + 3.0 * GELU_CUBIC * hidden * hidden
-                )
-                acc[0, k] = slope
-                zb[0, r, k] = acts[k]
-            zstep(0, 1)
-            for cp in ex0:
-                cp.wait_recv()
-            all_rows[0].first()
-    for k in range(2):
-        dhs.append((gate_col[k][:, 0:1] * acc[1, k] * acc[0, k]).astype(BF))
-        zb[1, r, k] = dhs[k]
-    zstep(1, 1)
-    zstep(0, 2)
-    for k in range(2):
-        gbuf[0, k] = lax.dot_general(
-            jnp.ones((8, F), F32), zb[0, r, k].astype(F32) * acc[1, k], (((1,), (1,)), ((), ())),
-            precision=lax.Precision.HIGHEST, preferred_element_type=F32,
-        )
-    g0 = send(gbuf.at[0], gsib, sib)
-
+    def step(a, d):
+        own_rows[a].done((d,))
+        for k in range(2):
+            total = None
+            for j in range(4):
+                px, py = (j, ys(d)) if k == 0 else (xs(d), j)
+                lhs = jnp.concatenate([xc[a, k, h, px, py] for h in range(2)], axis=1)
+                cols = pl.ds(pl.multiple_of((px * NY + py) * 2 * COL, 2 * COL), 2 * COL)
+                part = dot(lhs, win[k, cols, :]) if a == 0 else dot(lhs, wout[k, :, cols], 1, 1)
+                total = part if total is None else total + part
+            acc[a, k] = total if d == 0 else acc[a, k] + total
+
+    for sp in own_rows:
+        sp.first()
+    for sp in own_rows:
+        sp.second()
+    loads[2].wait()
+    loads[3].wait()
+    step(0, 0)
+    own_rows[0].forward()
+    step(1, 0)
+    own_rows[1].forward()
+    step(0, 3)
+    step(0, 1)
+    own_rows[0].last()
+    ex0 = exchange(0, lambda to: xc.at[0, x // 2, c, to // 2, two(to), slots])
+    ds[0, c, x, y, r] = xc[0, x // 2, c, r // 2, two(r), slots, :]
+    step(1, 3)
+    own_rows[1].last()
 
     @pl.loop(0, NX)
     def _(i):
@@ -317,6 +292,24 @@
 
     ex1 = exchange(1, lambda to: eb.at[to // 2, two(to)])
     ds[1, c, x, y, r] = eb[r // 2, two(r)]
+    step(0, 2)
+    for k in range(2):
+        hidden = acc[0, k]
+        tang = jnp.tanh(GELU_SCALE * (hidden + GELU_CUBIC * hidden * hidden * hidden))
+        slope = 0.5 * (1.0 + tang) + 0.5 * hidden * (1.0 - tang * tang) * GELU_SCALE * (
+            1.0 + 3.0 * GELU_CUBIC * hidden * hidden
+        )
+        acc[0, k] = slope
+        zb[0, r, k] = (0.5 * hidden * (1.0 + tang)).astype(BF)
+    zstep(0, 1)
+    step(1, 1)
+    for cp in ex0:
+        cp.wait_recv()
+    all_rows[0].first()
+    step(1, 2)
+    for k in range(2):
+        zb[1, r, k] = (gate_col[k][:, 0:1] * acc[1, k] * acc[0, k]).astype(BF)
+    zstep(1, 1)
 
     pair = []
     for k in range(2):
@@ -332,9 +325,14 @@
         pair.append(send(ps.at[k, oc], rsib.at[k], sib))
         if k == 0:
             all_rows[0].second()
-
-    all_rows[0].forward()
-    zstep(1, 2)
+            zstep(0, 2)
+
+    for k in range(2):
+        gbuf[0, k] = lax.dot_general(
+            jnp.ones((8, F), F32), zb[0, r, k].astype(F32) * acc[1, k], (((1,), (1,)), ((), ())),
+            precision=lax.Precision.HIGHEST, preferred_element_type=F32,
+        )
+    g0 = send(gbuf.at[0], gsib, sib)
 
     stage1 = [[], []]
     for k in range(2):
@@ -351,16 +349,18 @@
             else:
                 stage1[k].append(send(ps.at[1, c, :, ys(d)], rs1.at[1, y], dev(r, x, ys(d), c)))
 
-    zstep(0, 3)
+    zstep(1, 2)
+    for cp in ex1:
+        cp.wait_recv()
+    all_rows[1].first()
+    all_rows[0].forward()
 
     g0.wait_recv()
     gbuf[1] = gbuf[0] + gsib[...]
     gx[x] = gbuf[1]
     g1 = [send(gbuf.at[1], gx.at[x], dev(r, xs(d), y, c)) for d in (1, 3, 2)]
 
-    for cp in ex1:
-        cp.wait_recv()
-    all_rows[1].first()
+    zstep(0, 3)
     all_rows[0].last()
     zstep(1, 3)
 
@@ -418,24 +418,31 @@
         dgate_ref[0, k : k + 1, :] = total[k, 0:1, :]
 
     all_rows[1].last()
-    zstep(0, 5)
-    zstep(1, 5)
-    for sp in all_rows:
-        sp.done()
-    for k in range(2):
-        act = zb[0, :, k].reshape(NZ * CAP, F)
-        dh = zb[1, :, k].reshape(NZ * CAP, F)
-
-        def cols(a, j, h):
-            return jnp.concatenate(
+
+    def factor(w, k):
+        return zb[w, :, k].reshape(NZ * CAP, F)
+
+    def columns(a, k, j):
+        blocks = [
+            jnp.concatenate(
                 [ds[a, h, 2 * k : 2 * k + 2, :, g, j].reshape(CAP, COL) for g in range(NZ)], axis=0
             )
-
+            for h in range(2)
+        ]
+        return jnp.concatenate(blocks, axis=1)
+
+    zstep(1, 5)
+    all_rows[0].done()
+    for k in range(2):
         for j in range(2):
-            xk = jnp.concatenate([cols(0, j, h) for h in range(2)], axis=1)
-            sk = jnp.concatenate([cols(1, j, h) for h in range(2)], axis=1)
-            dwin_ref[k, j * 256 : (j + 1) * 256, :] = dot(xk, dh, 0, 0).astype(BF)
-            dwout_ref[k, :, j * 256 : (j + 1) * 256] = dot(act, sk, 0, 0).astype(BF)
+            at = slice(j * 2 * COL, (j + 1) * 2 * COL)
+            dwin_ref[k, at, :] = dot(columns(0, k, j), factor(1, k), 0, 0).astype(BF)
+    zstep(0, 5)
+    all_rows[1].done()
+    for k in range(2):
+        for j in range(2):
+            at = slice(j * 2 * COL, (j + 1) * 2 * COL)
+            dwout_ref[k, :, at] = dot(factor(0, k), columns(1, k, j), 0, 0).astype(BF)
 
     for cp in back:
         cp.wait_recv()

time: 81.3 us -> 78.4 us (0.964)
  Pallas kernels: 80.5 us -> 77.6 us
    pallas_call x1, Pallas kernels: 77.6 us -> 74.6 us  [local(): pl.pallas_call(kernel, out_shape=(jax.ShapeDtypeStruct((2, NX, NY, ROWS,...]
where the time goes in v4:
time: 78.4 us; the launch traced here: 78.2 us
  Pallas kernels  77.6 us (99%)
    pallas_call x1, Pallas kernels, local(): pl.pallas_call(kernel, out_shape=(jax.ShapeDtypeStruct((2, NX, NY, ROWS,...  74.6 us
    pallas_call x1, Pallas kernels, local(): pl.pallas_call(finish, out_shape=(jax.ShapeDtypeStruct((1, TOK, D), BF),...  2.94 us

profile of v4, /device:TPU:1, one launch (start us, length us, event | category | flops | bytes accessed | tf_op | source)
XLA Modules:
  0.0 78.2 jit_solution(6578174954480108871)
XLA Ops:
  0.6 74.6 %expert_backward.1 = (bf16[2,4,4,16,128]{4,3,2,1,0:T(8,128)(2,1)}, bf16[128,16]{1,0:T(8,128)(2,1)}, f32[1,2,128]{2,1,0:T(2,128)}, bf16[2,512,256]{2,1,0:T(8,128)(2,1)}, bf16[2,256,512]{2,1,0:T(8,128)(2,1)}) custom-call(bf16[1,128,4096]{2,1,0:T(8,128)(2,1)} %tok_hbm.1, bf16[1,128,4096]{2,1,0:T(8,128)(2,1)} %grad_hbm.1, f32[1,2,128]{2,1,0:T(2,128)} %gates_ref.1, ...), custom_call_target="tpu_custom_call" | custom-call | tf_op jit(solution)/shard_map/expert_backward/pallas_call | solution.py:475
  75.3 2.9 %finish.1 = (bf16[1,128,4096]{2,1,0:T(8,128)(2,1)}, f32[1,2,128]{2,1,0:T(2,128)}, bf16[2,512,256]{2,1,0:T(8,128)(2,1)}, bf16[2,256,512]{2,1,0:T(8,128)(2,1)}) custom-call(bf16[2,4,4,16,128]{4,3,2,1,0:T(8,128)(2,1)} %get-tuple-element.9.rows_ref, bf16[128,16]{1,0:T(8,128)(2,1)} %get-tuple-element.10.unpick_ref, f32[1,2,128]{2,1,0:T(2,128)} %get-tuple-element.11.gate_ref, ...), custom_call_target="tpu_custom_call" | custom-call | tf_op jit(solution)/shard_map/finish/pallas_call | solution.py:523

commit v5 on v4

--- a/solution.py
+++ b/solution.py
@@ -26,6 +26,10 @@
 
 NSEM = 144
 
+ORDER = (
+    ("slot", 0), ("cols", 0, 2), ("ring", 0, 2), ("slot", 1), ("cols", 1, 1), ("gate", 0), ("pair", 0), ("pair", 1), ("ring", 1, 2), ("cols", 0, 3), ("cols", 1, 2), ("gate", 1), ("ring", 0, 3), ("ring", 1, 3), ("sum", 0), ("sum", 1), ("ring", 0, 4), ("cols", 0, 4), ("gate", 2), ("ring", 1, 4), ("cols", 1, 3), ("back",), ("pick",), ("gate", 3), ("cols", 1, 4),
+)
+
 
 def dot(a, b, ca=1, cb=0):
     return lax.dot_general(a, b, (((ca,), (cb,)), ((), ())), preferred_element_type=F32)
@@ -33,10 +37,10 @@
 
 def kernel(
     tok_hbm, grad_hbm, gates_ref, chosen_ref, win_hbm, wout_hbm,
-    rows_ref, unpick_ref, dgate_ref, dwin_ref, dwout_ref,
-    tok, grad, win, wout, pk, rp, xc, gc, eb, ds, zb, acc, ps, rsib, rs1, ts, rs2, ob, rb,
+    rows_hbm, unpick_hbm, dgate_hbm, dwin_hbm, dwout_hbm,
+    unpick_ref, dgate_ref, dwin_ref, dwout_ref, tok, grad, win, wout, pk, rp, xc, gc, eb, ds, zb, acc, ps, rsib, rs1, ts, rs2, ob, rb,
     gbuf, gsib, gx, gy,
-    ssem, rsem, asem, arsem, bsem, brsem, lsem,
+    ssem, rsem, asem, arsem, bsem, brsem, lsem, osem,
 ):
     r = lax.axis_index("rep")
     e = lax.axis_index("exp")
@@ -283,16 +287,8 @@
     ex0 = exchange(0, lambda to: xc.at[0, x // 2, c, to // 2, two(to), slots])
     ds[0, c, x, y, r] = xc[0, x // 2, c, r // 2, two(r), slots, :]
     step(1, 3)
+    step(0, 2)
     own_rows[1].last()
-
-    @pl.loop(0, NX)
-    def _(i):
-        for j in range(NY):
-            eb[i, j] = (gc[chip] * xc[1, x // 2, c, i, j, slots, :].astype(F32)).astype(BF)
-
-    ex1 = exchange(1, lambda to: eb.at[to // 2, two(to)])
-    ds[1, c, x, y, r] = eb[r // 2, two(r)]
-    step(0, 2)
     for k in range(2):
         hidden = acc[0, k]
         tang = jnp.tanh(GELU_SCALE * (hidden + GELU_CUBIC * hidden * hidden * hidden))
@@ -303,6 +299,14 @@
         zb[0, r, k] = (0.5 * hidden * (1.0 + tang)).astype(BF)
     zstep(0, 1)
     step(1, 1)
+
+    @pl.loop(0, NX)
+    def _(i):
+        for j in range(NY):
+            eb[i, j] = (gc[chip] * xc[1, x // 2, c, i, j, slots, :].astype(F32)).astype(BF)
+
+    ex1 = exchange(1, lambda to: eb.at[to // 2, two(to)])
+    ds[1, c, x, y, r] = eb[r // 2, two(r)]
     for cp in ex0:
         cp.wait_recv()
     all_rows[0].first()
@@ -310,32 +314,26 @@
     for k in range(2):
         zb[1, r, k] = (gate_col[k][:, 0:1] * acc[1, k] * acc[0, k]).astype(BF)
     zstep(1, 1)
-
-    pair = []
-    for k in range(2):
-
+    pair, stage1, stage2, gates_on_way, kept = {}, {0: [], 1: []}, {0: [], 1: []}, {}, {}
+    outs = []
+
+    def leave(src, dst):
+        cp = pltpu.make_async_copy(src, dst, osem.at[len(outs)])
+        cp.start()
+        outs.append(cp)
+
+    def slot_part(k):
         @pl.loop(0, NX)
         def _(i):
             cols = pl.ds(pl.multiple_of(i * BLK, BLK), BLK)
-            part = dot(zb[1, r, k], win[k, cols, :], 1, 1).astype(BF)
+            part = dot(win[k, cols, :], zb[1, r, k], 1, 1).astype(BF)
             for j in range(NY):
                 for h in range(2):
-                    ps[k, h, i, j] = part[:, (2 * j + h) * COL : (2 * j + h + 1) * COL]
-
-        pair.append(send(ps.at[k, oc], rsib.at[k], sib))
-        if k == 0:
-            all_rows[0].second()
-            zstep(0, 2)
-
-    for k in range(2):
-        gbuf[0, k] = lax.dot_general(
-            jnp.ones((8, F), F32), zb[0, r, k].astype(F32) * acc[1, k], (((1,), (1,)), ((), ())),
-            precision=lax.Precision.HIGHEST, preferred_element_type=F32,
-        )
-    g0 = send(gbuf.at[0], gsib, sib)
-
-    stage1 = [[], []]
-    for k in range(2):
+                    ps[k, h, i, j] = part[(2 * j + h) * COL : (2 * j + h + 1) * COL]
+
+        pair[k] = send(ps.at[k, oc], rsib.at[k], sib)
+
+    def pair_sum(k):
         pair[k].wait_recv()
 
         @pl.loop(0, NX)
@@ -349,23 +347,7 @@
             else:
                 stage1[k].append(send(ps.at[1, c, :, ys(d)], rs1.at[1, y], dev(r, x, ys(d), c)))
 
-    zstep(1, 2)
-    for cp in ex1:
-        cp.wait_recv()
-    all_rows[1].first()
-    all_rows[0].forward()
-
-    g0.wait_recv()
-    gbuf[1] = gbuf[0] + gsib[...]
-    gx[x] = gbuf[1]
-    g1 = [send(gbuf.at[1], gx.at[x], dev(r, xs(d), y, c)) for d in (1, 3, 2)]
-
-    zstep(0, 3)
-    all_rows[0].last()
-    zstep(1, 3)
-
-    stage2 = [[], []]
-    for k in range(2):
+    def first_sum(k):
         for cp in stage1[k]:
             cp.wait_recv()
         for j in range(4):
@@ -379,45 +361,71 @@
             else:
                 stage2[k].append(send(ts.at[1, xs(d)], rs2.at[1, x], dev(r, xs(d), y, c)))
 
-    all_rows[1].second()
-    zstep(0, 4)
-    for cp in g1:
-        cp.wait_recv()
-    gbuf[2] = (gx[0] + gx[1]) + (gx[2] + gx[3])
-    gy[y] = gbuf[2]
-    g2 = [send(gbuf.at[2], gy.at[y], dev(r, x, ys(d), c)) for d in (1, 3, 2)]
-
-    expand = jnp.concatenate([hot(pos_row[k] == iota((PAD, CAP), 0)) for k in range(2)], axis=1)
-    sums = []
-    for k in range(2):
-        for cp in stage2[k]:
+    def return_rows():
+        expand = jnp.concatenate([hot(pos_row[k] == iota((PAD, CAP), 0)) for k in range(2)], axis=1)
+        sums = []
+        for k in range(2):
+            for cp in stage2[k]:
+                cp.wait_recv()
+            total = ts[k, y if k == 0 else x].astype(F32)
+            for d in (1, 2, 3):
+                total += rs2[k, ys(d) if k == 0 else xs(d)].astype(F32)
+            sums.append(total.astype(BF))
+        sums = jnp.concatenate(sums, axis=1)
+        ob[...] = dot(expand, sums, 1, 1).astype(BF).reshape(2, NX, NY, ROWS, COL)
+        kept["back"] = plane(ob, rb, bsem, brsem)
+        rb[c, x, y] = ob[c, x, y]
+
+    def gate_sum(n):
+        if n == 0:
+            for k in range(2):
+                gbuf[0, k] = lax.dot_general(
+                    jnp.ones((8, F), F32), zb[0, r, k].astype(F32) * acc[1, k], (((1,), (1,)), ((), ())),
+                    precision=lax.Precision.HIGHEST, preferred_element_type=F32,
+                )
+            gates_on_way[0] = [send(gbuf.at[0], gsib, sib)]
+            return
+        for cp in gates_on_way[n - 1]:
             cp.wait_recv()
-        total = ts[k, y if k == 0 else x].astype(F32)
-        for d in (1, 2, 3):
-            total += rs2[k, ys(d) if k == 0 else xs(d)].astype(F32)
-        sums.append(total.astype(BF))
-    ob[...] = dot(expand, jnp.concatenate(sums, axis=0)).astype(BF).reshape(2, NX, NY, ROWS, COL)
-
-    back = plane(ob, rb, bsem, brsem)
-    rb[c, x, y] = ob[c, x, y]
-    zstep(1, 4)
-
-    all_rows[1].forward()
-
-    unpick = jnp.zeros((TOK, ROWS), F32)
-    for k in range(2):
-        bt = hot(ch_row[k] - e * TOK == iota((TOK, CAP), 0))
-        at = hot(pos_col[k] - my_first == iota((CAP, ROWS), 1))
-        unpick += dot(bt, at)
-    unpick_ref[...] = unpick.astype(BF)
-
-    for cp in g2:
-        cp.wait_recv()
-    total = (gy[0] + gy[1]) + (gy[2] + gy[3])
-    for k in range(2):
-        dgate_ref[0, k : k + 1, :] = total[k, 0:1, :]
-
-    all_rows[1].last()
+        if n == 1:
+            gbuf[1] = gbuf[0] + gsib[...]
+            gx[x] = gbuf[1]
+            gates_on_way[1] = [send(gbuf.at[1], gx.at[x], dev(r, xs(d), y, c)) for d in (1, 3, 2)]
+        elif n == 2:
+            gbuf[2] = (gx[0] + gx[1]) + (gx[2] + gx[3])
+            gy[y] = gbuf[2]
+            gates_on_way[2] = [send(gbuf.at[2], gy.at[y], dev(r, x, ys(d), c)) for d in (1, 3, 2)]
+        else:
+            total = (gy[0] + gy[1]) + (gy[2] + gy[3])
+            for k in range(2):
+                dgate_ref[0, k : k + 1, :] = total[k, 0:1, :]
+            leave(dgate_ref, dgate_hbm)
+
+    def column_spread(a, n):
+        sp = all_rows[a]
+        if n == 1:
+            if a == 1:
+                for cp in ex1:
+                    cp.wait_recv()
+            sp.first()
+        else:
+            (None, None, sp.second, sp.forward, sp.last)[n]()
+
+    def owner_pick():
+        unpick = jnp.zeros((TOK, ROWS), F32)
+        for k in range(2):
+            bt = hot(ch_row[k] - e * TOK == iota((TOK, CAP), 0))
+            at = hot(pos_col[k] - my_first == iota((CAP, ROWS), 1))
+            unpick += dot(bt, at)
+        unpick_ref[...] = unpick.astype(BF)
+        leave(unpick_ref, unpick_hbm)
+
+    steps = {
+        "slot": slot_part, "pair": pair_sum, "sum": first_sum, "back": return_rows, "gate": gate_sum,
+        "ring": zstep, "cols": column_spread, "pick": owner_pick,
+    }
+    for name, *at in ORDER:
+        steps[name](*at)
 
     def factor(w, k):
         return zb[w, :, k].reshape(NZ * CAP, F)
@@ -437,32 +445,60 @@
         for j in range(2):
             at = slice(j * 2 * COL, (j + 1) * 2 * COL)
             dwin_ref[k, at, :] = dot(columns(0, k, j), factor(1, k), 0, 0).astype(BF)
+    leave(dwin_ref, dwin_hbm)
     zstep(0, 5)
     all_rows[1].done()
     for k in range(2):
         for j in range(2):
             at = slice(j * 2 * COL, (j + 1) * 2 * COL)
             dwout_ref[k, :, at] = dot(factor(0, k), columns(1, k, j), 0, 0).astype(BF)
-
-    for cp in back:
+    leave(dwout_ref, dwout_hbm)
+
+    for cp in kept["back"]:
         cp.wait_recv()
-    rows_ref[...] = rb[...]
+    leave(rb, rows_hbm)
 
     assert counter[0] <= NSEM, counter[0]
     for cp in sent:
         cp.wait_send()
 
-    for cp in forth + back:
+    for cp in forth + kept["back"]:
         cp.wait_send()
-
-
-def finish(rows_ref, unpick_ref, gate_ref, win_ref, wout_ref, dtok_ref, dgate_ref, dwin_ref, dwout_ref):
+    for cp in outs:
+        cp.wait()
+
+
+def finish(
+    rows_hbm, unpick_hbm, gate_hbm, win_hbm, wout_hbm, dtok_hbm, dgate_hbm, dwin_hbm, dwout_hbm,
+    rows, unpick, gate, win, wout, dtok, isem, osem,
+):
+    ins = [
+        pltpu.make_async_copy(src, dst, isem.at[i])
+        for i, (src, dst) in enumerate(
+            ((rows_hbm, rows), (unpick_hbm, unpick), (gate_hbm, gate), (win_hbm, win), (wout_hbm, wout))
+        )
+    ]
+    for cp in ins:
+        cp.start()
+    outs = []
+
+    def leave(src, dst):
+        cp = pltpu.make_async_copy(src, dst, osem.at[len(outs)])
+        cp.start()
+        outs.append(cp)
+
+    ins[0].wait()
+    ins[1].wait()
     for i in range(NX):
-        rows = jnp.concatenate([rows_ref[h, i, j] for j in range(NY) for h in range(2)], axis=1)
-        dtok_ref[0, :, i * BLK : (i + 1) * BLK] = dot(unpick_ref[...], rows).astype(BF)
-    dgate_ref[...] = gate_ref[...]
-    dwin_ref[...] = win_ref[...]
-    dwout_ref[...] = wout_ref[...]
+        block = jnp.concatenate([rows[h, i, j] for j in range(NY) for h in range(2)], axis=1)
+        at = pl.ds(i * BLK, BLK)
+        dtok[0, :, at] = dot(unpick[...], block).astype(BF)
+        leave(dtok.at[0, :, at], dtok_hbm.at[0, :, at])
+    for cp, src, dst in zip(ins[2:], (gate, win, wout), (dgate_hbm, dwin_hbm, dwout_hbm)):
+        cp.wait()
+        leave(src, dst)
+    for cp in outs:
+        cp.wait()
 
 
 def local(tokens, grad_out, gates, chosen, w_in, w_out):
@@ -482,8 +518,12 @@
             d_out,
         ),
         in_specs=[hbm, hbm, vmem, vmem, hbm, hbm],
-        out_specs=(vmem,) * 5,
+        out_specs=(hbm,) * 5,
         scratch_shapes=[
+            pltpu.VMEM((TOK, ROWS), BF),
+            pltpu.VMEM((1, 2, CAP), F32),
+            pltpu.VMEM((2, D // NZ, F), BF),
+            pltpu.VMEM((2, F, D // NZ), BF),
             pltpu.VMEM((TOK, D), BF),
             pltpu.VMEM((TOK, D), BF),
             pltpu.VMEM((2, D, F), BF),
@@ -514,6 +554,7 @@
             dma((PLANE,)),
             dma((PLANE,)),
             dma((4,)),
+            dma((5,)),
         ],
         compiler_params=pltpu.CompilerParams(
             collective_id=0, has_side_effects=True, vmem_limit_bytes=60 << 20
@@ -523,8 +564,18 @@
     return pl.pallas_call(
         finish,
         out_shape=(jax.ShapeDtypeStruct((1, TOK, D), BF), d_gate, d_in, d_out),
-        in_specs=[vmem] * 5,
-        out_specs=(vmem,) * 4,
+        in_specs=[hbm] * 5,
+        out_specs=(hbm,) * 4,
+        scratch_shapes=[
+            pltpu.VMEM((2, NX, NY, ROWS, COL), BF),
+            pltpu.VMEM((TOK, ROWS), BF),
+            pltpu.VMEM((1, 2, CAP), F32),
+            pltpu.VMEM((2, D // NZ, F), BF),
+            pltpu.VMEM((2, F, D // NZ), BF),
+            pltpu.VMEM((1, TOK, D), BF),
+            dma((5,)),
+            dma((7,)),
+        ],
         compiler_params=pltpu.CompilerParams(vmem_limit_bytes=60 << 20),
         name="finish",
     )(*parts)

time: 78.4 us -> 72.7 us (0.927)
  Pallas kernels: 77.6 us -> 71.9 us
    pallas_call x1, Pallas kernels: 74.6 us -> 69.4 us  [local(): pl.pallas_call(kernel, out_shape=(jax.ShapeDtypeStruct((2, NX, NY, ROWS,...]
where the time goes in v5:
time: 72.7 us; the launch traced here: 72.6 us
  Pallas kernels  71.9 us (99%)
    pallas_call x1, Pallas kernels, local(): pl.pallas_call(kernel, out_shape=(jax.ShapeDtypeStruct((2, NX, NY, ROWS,...  69.4 us
    pallas_call x1, Pallas kernels, local(): pl.pallas_call(finish, out_shape=(jax.ShapeDtypeStruct((1, TOK, D), BF),...  2.53 us

profile of v5, /device:TPU:1, one launch (start us, length us, event | category | flops | bytes accessed | tf_op | source)
XLA Modules:
  0.0 72.6 jit_solution(4907843916579283215)
XLA Ops:
  0.6 69.4 %expert_backward.1 = (bf16[2,4,4,16,128]{4,3,2,1,0:T(8,128)(2,1)}, bf16[128,16]{1,0:T(8,128)(2,1)}, f32[1,2,128]{2,1,0:T(2,128)}, bf16[2,512,256]{2,1,0:T(8,128)(2,1)}, bf16[2,256,512]{2,1,0:T(8,128)(2,1)}) custom-call(bf16[1,128,4096]{2,1,0:T(8,128)(2,1)} %tok_hbm.1, bf16[1,128,4096]{2,1,0:T(8,128)(2,1)} %grad_hbm.1, f32[1,2,128]{2,1,0:T(2,128)} %gates_ref.1, ...), custom_call_target="tpu_custom_call" | custom-call | tf_op jit(solution)/shard_map/expert_backward/pallas_call | solution.py:511
  70.1 2.5 %finish.1 = (bf16[1,128,4096]{2,1,0:T(8,128)(2,1)}, f32[1,2,128]{2,1,0:T(2,128)}, bf16[2,512,256]{2,1,0:T(8,128)(2,1)}, bf16[2,256,512]{2,1,0:T(8,128)(2,1)}) custom-call(bf16[2,4,4,16,128]{4,3,2,1,0:T(8,128)(2,1)} %get-tuple-element.9.rows_hbm, bf16[128,16]{1,0:T(8,128)(2,1)} %get-tuple-element.10.unpick_hbm, f32[1,2,128]{2,1,0:T(2,128)} %get-tuple-element.11.gate_hbm, ...), custom_call_target="tpu_custom_call" | custom-call | tf_op jit(solution)/shard_map/finish/pallas_call | solution.py:564

commit v6 on v5

--- a/solution.py
+++ b/solution.py
@@ -27,7 +27,7 @@
 NSEM = 144
 
 ORDER = (
-    ("slot", 0), ("cols", 0, 2), ("ring", 0, 2), ("slot", 1), ("cols", 1, 1), ("gate", 0), ("pair", 0), ("pair", 1), ("ring", 1, 2), ("cols", 0, 3), ("cols", 1, 2), ("gate", 1), ("ring", 0, 3), ("ring", 1, 3), ("sum", 0), ("sum", 1), ("ring", 0, 4), ("cols", 0, 4), ("gate", 2), ("ring", 1, 4), ("cols", 1, 3), ("back",), ("pick",), ("gate", 3), ("cols", 1, 4),
+    ("cols", 2), ("slot", 0), ("ring", 0, 2), ("slot", 1), ("gate", 0), ("pair", 0), ("pair", 1), ("ring", 1, 2), ("cols", 3), ("gate", 1), ("ring", 0, 3), ("ring", 1, 3), ("sum", 0), ("sum", 1), ("ring", 0, 4), ("gate", 2), ("ring", 1, 4), ("cols", 4), ("back",), ("pick",), ("gate", 3),
 )
 
 
@@ -38,9 +38,9 @@
 def kernel(
     tok_hbm, grad_hbm, gates_ref, chosen_ref, win_hbm, wout_hbm,
     rows_hbm, unpick_hbm, dgate_hbm, dwin_hbm, dwout_hbm,
-    unpick_ref, dgate_ref, dwin_ref, dwout_ref, tok, grad, win, wout, pk, rp, xc, gc, eb, ds, zb, acc, ps, rsib, rs1, ts, rs2, ob, rb,
+    unpick_ref, dgate_ref, dwin_ref, dwout_ref, tok, grad, win, wout, pk, rp, xc, cross_out, xd, zb, acc, ps, rsib, rs1, ts, rs2, ob, rb, rows_out,
     gbuf, gsib, gx, gy,
-    ssem, rsem, asem, arsem, bsem, brsem, lsem, osem,
+    ssem, rsem, asem, arsem, bsem, brsem, lsem, osem, csem,
 ):
     r = lax.axis_index("rep")
     e = lax.axis_index("exp")
@@ -81,6 +81,11 @@
     for d in range(1, NZ):
         pl.semaphore_signal(barrier, inc=1, device_id=dev(zs(d), x, y, c), device_id_type=MESH)
 
+    m = e // 4
+    away = m != 0
+
+    def turned(p):
+        return lax.rem(p + 2 * r, NX * NY)
     counter = [0]
     sent = []
 
@@ -132,18 +137,21 @@
     loads[2].start()
     loads[3].start()
 
+    def wide(p):
+        return pl.ds(pl.multiple_of(turned(p) * 2 * COL, 2 * COL), 2 * COL)
+
     @pl.loop(0, NX)
     def _(i):
-        cols = pl.ds(pl.multiple_of(i * BLK, BLK), BLK)
-        xr = dot(pick, tok[:, cols]).astype(BF)
-        dr = dot(pick, grad[:, cols]).astype(BF)
         for j in range(NY):
+            cols = wide(i * NY + j)
+            xr = dot(pick, tok[:, cols]).astype(BF)
+            dr = dot(pick, grad[:, cols]).astype(BF)
             for k in range(2):
-                at = slice((2 * j + k) * COL, (2 * j + k + 1) * COL)
-                pk[k, i, j, 0] = xr[:, at]
-                pk[k, i, j, 1] = dr[:, at]
+                pk[k, i, j, 0] = xr[:, k * COL : (k + 1) * COL]
+                pk[k, i, j, 1] = dr[:, k * COL : (k + 1) * COL]
 
     pl.semaphore_wait(barrier, PLANE - 1 + NZ - 1)
+
 
     def plane(src, dst, s_sem, r_sem):
         copies = []
@@ -162,16 +170,17 @@
     gather = jnp.concatenate([hot(pos_col[k] == iota((CAP, PAD), 1)) for k in range(2)], axis=0)
     for k in range(2):
         gate_col.append(jnp.broadcast_to(gates_ref[0, k : k + 1, :], sq).T)
-        gc[k * 8 : (k + 1) * 8] = gate_col[k].reshape(8, ROWS, COL)
 
     for cp in forth:
         cp.wait_recv()
 
     both = jnp.concatenate([rp[:, :, :, k].reshape(PAD, COL) for k in range(2)], axis=1)
-    both = dot(gather, both).astype(BF)
+    both = dot(gather, both)
     for a in range(2):
         for k in range(2):
-            xc[a, k, c, x, y] = both[k * CAP : (k + 1) * CAP, a * COL : (a + 1) * COL]
+            block = both[k * CAP : (k + 1) * CAP, a * COL : (a + 1) * COL]
+            xc[a, k, c, x, y] = block.astype(BF)
+            cross_out[k, a] = (block if a == 0 else gate_col[k] * block).astype(BF)
 
     class Spread:
         def __init__(self, row):
@@ -228,21 +237,16 @@
     def rows_of(a):
         return lambda k, d, at: xc.at[a, 0, c, at, ys(d)] if k == 0 else xc.at[a, 1, c, xs(d), at]
 
-    def columns_of(a):
-        return lambda k, d, at: ds.at[a, c, at, ys(d), 0:4] if k == 0 else ds.at[a, c, xs(d), at, 4:8]
+    def columns(k, d, at):
+        return xd.at[0, c, at, ys(d)] if k == 0 else xd.at[1, c, xs(d), at]
 
     own_rows = [Spread(rows_of(a)) for a in range(2)]
-    all_rows = [Spread(columns_of(a)) for a in range(2)]
-    slots = pl.ds(pl.multiple_of(lax.rem(chip, 8) * ROWS, ROWS), ROWS)
-
-    def two(to):
-        return pl.ds(2 * lax.rem(to, 2), 2)
-
-    def exchange(a, src):
-        copies = []
-        for d in (1, 7, 2, 6, 3, 5, 4):
-            copies.append(send(src(zs(d)), ds.at[a, c, x, y, r], dev(zs(d), x, y, c)))
-        return copies
+    all_rows = Spread(columns)
+
+    cross = pltpu.make_async_remote_copy(
+        src_ref=cross_out, dst_ref=xd.at[:, c, x, y], send_sem=csem.at[0], recv_sem=csem.at[1],
+        device_id=(zs(m), e), device_id_type=MESH,
+    )
 
     right, left = dev(zs(1), x, y, c), dev(zs(7), x, y, c)
     ring = [None, None]
@@ -266,13 +270,22 @@
             for j in range(4):
                 px, py = (j, ys(d)) if k == 0 else (xs(d), j)
                 lhs = jnp.concatenate([xc[a, k, h, px, py] for h in range(2)], axis=1)
-                cols = pl.ds(pl.multiple_of((px * NY + py) * 2 * COL, 2 * COL), 2 * COL)
+                cols = wide(px * NY + py)
                 part = dot(lhs, win[k, cols, :]) if a == 0 else dot(lhs, wout[k, :, cols], 1, 1)
                 total = part if total is None else total + part
             acc[a, k] = total if d == 0 else acc[a, k] + total
 
     for sp in own_rows:
         sp.first()
+
+    @pl.when(away)
+    def _():
+        cross.start()
+
+    @pl.when(jnp.logical_not(away))
+    def _():
+        xd[:, c, x, y] = cross_out[...]
+
     for sp in own_rows:
         sp.second()
     loads[2].wait()
@@ -281,11 +294,15 @@
     own_rows[0].forward()
     step(1, 0)
     own_rows[1].forward()
+
+    @pl.when(away)
+    def _():
+        cross.wait_recv()
+
+    all_rows.first()
     step(0, 3)
     step(0, 1)
     own_rows[0].last()
-    ex0 = exchange(0, lambda to: xc.at[0, x // 2, c, to // 2, two(to), slots])
-    ds[0, c, x, y, r] = xc[0, x // 2, c, r // 2, two(r), slots, :]
     step(1, 3)
     step(0, 2)
     own_rows[1].last()
@@ -299,17 +316,6 @@
         zb[0, r, k] = (0.5 * hidden * (1.0 + tang)).astype(BF)
     zstep(0, 1)
     step(1, 1)
-
-    @pl.loop(0, NX)
-    def _(i):
-        for j in range(NY):
-            eb[i, j] = (gc[chip] * xc[1, x // 2, c, i, j, slots, :].astype(F32)).astype(BF)
-
-    ex1 = exchange(1, lambda to: eb.at[to // 2, two(to)])
-    ds[1, c, x, y, r] = eb[r // 2, two(r)]
-    for cp in ex0:
-        cp.wait_recv()
-    all_rows[0].first()
     step(1, 2)
     for k in range(2):
         zb[1, r, k] = (gate_col[k][:, 0:1] * acc[1, k] * acc[0, k]).astype(BF)
@@ -325,11 +331,10 @@
     def slot_part(k):
         @pl.loop(0, NX)
         def _(i):
-            cols = pl.ds(pl.multiple_of(i * BLK, BLK), BLK)
-            part = dot(win[k, cols, :], zb[1, r, k], 1, 1).astype(BF)
             for j in range(NY):
+                part = dot(win[k, wide(i * NY + j), :], zb[1, r, k], 1, 1).astype(BF)
                 for h in range(2):
-                    ps[k, h, i, j] = part[(2 * j + h) * COL : (2 * j + h + 1) * COL]
+                    ps[k, h, i, j] = part[h * COL : (h + 1) * COL]
 
         pair[k] = send(ps.at[k, oc], rsib.at[k], sib)
 
@@ -401,15 +406,8 @@
                 dgate_ref[0, k : k + 1, :] = total[k, 0:1, :]
             leave(dgate_ref, dgate_hbm)
 
-    def column_spread(a, n):
-        sp = all_rows[a]
-        if n == 1:
-            if a == 1:
-                for cp in ex1:
-                    cp.wait_recv()
-            sp.first()
-        else:
-            (None, None, sp.second, sp.forward, sp.last)[n]()
+    def column_spread(n):
+        (None, None, all_rows.second, all_rows.forward, all_rows.last)[n]()
 
     def owner_pick():
         unpick = jnp.zeros((TOK, ROWS), F32)
@@ -428,26 +426,23 @@
         steps[name](*at)
 
     def factor(w, k):
-        return zb[w, :, k].reshape(NZ * CAP, F)
+        return jnp.concatenate([zb[w, zs((NZ - g) % NZ), k] for g in range(NZ)], axis=0)
 
     def columns(a, k, j):
         blocks = [
-            jnp.concatenate(
-                [ds[a, h, 2 * k : 2 * k + 2, :, g, j].reshape(CAP, COL) for g in range(NZ)], axis=0
-            )
+            jnp.concatenate([xd[k, h, g // 2, 2 * (g % 2) + j, a] for g in range(NZ)], axis=0)
             for h in range(2)
         ]
         return jnp.concatenate(blocks, axis=1)
 
     zstep(1, 5)
-    all_rows[0].done()
+    all_rows.done()
     for k in range(2):
         for j in range(2):
             at = slice(j * 2 * COL, (j + 1) * 2 * COL)
             dwin_ref[k, at, :] = dot(columns(0, k, j), factor(1, k), 0, 0).astype(BF)
     leave(dwin_ref, dwin_hbm)
     zstep(0, 5)
-    all_rows[1].done()
     for k in range(2):
         for j in range(2):
             at = slice(j * 2 * COL, (j + 1) * 2 * COL)
@@ -456,7 +451,14 @@
 
     for cp in kept["back"]:
         cp.wait_recv()
-    leave(rb, rows_hbm)
+
+    @pl.loop(0, NX)
+    def _(i):
+        for j in range(NY):
+            to = turned(i * NY + j)
+            rows_out[:, to // NY, lax.rem(to, NY)] = rb[:, i, j]
+
+    leave(rows_out, rows_hbm)
 
     assert counter[0] <= NSEM, counter[0]
     for cp in sent:
@@ -466,6 +468,10 @@
         cp.wait_send()
     for cp in outs:
         cp.wait()
+
+    @pl.when(away)
+    def _():
+        cross.wait_send()
 
 
 def finish(
@@ -531,9 +537,8 @@
             pltpu.VMEM((2, NX, NY, 2, ROWS, COL), BF),
             pltpu.VMEM((2, NX, NY, 2, ROWS, COL), BF),
             pltpu.VMEM((2, 2, 2, NX, NY, CAP, COL), BF),
-            pltpu.VMEM((NX * NY, ROWS, COL), F32),
-            pltpu.VMEM((NX, NY, ROWS, COL), BF),
-            pltpu.VMEM((2, 2, NX, NY, NZ, 2, ROWS, COL), BF),
+            pltpu.VMEM((2, 2, CAP, COL), BF),
+            pltpu.VMEM((2, 2, NX, NY, 2, CAP, COL), BF),
             pltpu.VMEM((2, NZ, 2, CAP, F), BF),
             pltpu.VMEM((2, 2, CAP, F), F32),
             pltpu.VMEM((2, 2, NX, NY, CAP, COL), BF),
@@ -541,6 +546,7 @@
             pltpu.VMEM((2, 4, 4, CAP, COL), BF),
             pltpu.VMEM((2, 4, CAP, COL), BF),
             pltpu.VMEM((2, 4, CAP, COL), BF),
+            pltpu.VMEM((2, NX, NY, ROWS, COL), BF),
             pltpu.VMEM((2, NX, NY, ROWS, COL), BF),
             pltpu.VMEM((2, NX, NY, ROWS, COL), BF),
             pltpu.VMEM((3, 2, 8, CAP), F32),
@@ -555,6 +561,7 @@
             dma((PLANE,)),
             dma((4,)),
             dma((5,)),
+            dma((2,)),
         ],
         compiler_params=pltpu.CompilerParams(
             collective_id=0, has_side_effects=True, vmem_limit_bytes=60 << 20

time: 72.7 us -> 70.2 us (0.966)
  Pallas kernels: 71.9 us -> 69.4 us
    pallas_call x1, Pallas kernels: 69.4 us -> 66.9 us  [local(): pl.pallas_call(kernel, out_shape=(jax.ShapeDtypeStruct((2, NX, NY, ROWS,...]
where the time goes in v6:
time: 70.2 us; the launch traced here: 70.1 us
  Pallas kernels  69.4 us (99%)
    pallas_call x1, Pallas kernels, local(): pl.pallas_call(kernel, out_shape=(jax.ShapeDtypeStruct((2, NX, NY, ROWS,...  66.9 us
    pallas_call x1, Pallas kernels, local(): pl.pallas_call(finish, out_shape=(jax.ShapeDtypeStruct((1, TOK, D), BF),...  2.52 us

profile of v6, /device:TPU:1, one launch (start us, length us, event | category | flops | bytes accessed | tf_op | source)
XLA Modules:
  0.0 70.1 jit_solution(2344821924833096029)
XLA Ops:
  0.6 66.9 %expert_backward.1 = (bf16[2,4,4,16,128]{4,3,2,1,0:T(8,128)(2,1)}, bf16[128,16]{1,0:T(8,128)(2,1)}, f32[1,2,128]{2,1,0:T(2,128)}, bf16[2,512,256]{2,1,0:T(8,128)(2,1)}, bf16[2,256,512]{2,1,0:T(8,128)(2,1)}) custom-call(bf16[1,128,4096]{2,1,0:T(8,128)(2,1)} %tok_hbm.1, bf16[1,128,4096]{2,1,0:T(8,128)(2,1)} %grad_hbm.1, f32[1,2,128]{2,1,0:T(2,128)} %gates_ref.1, ...), custom_call_target="tpu_custom_call" | custom-call | tf_op jit(solution)/shard_map/expert_backward/pallas_call | solution.py:517
  67.6 2.5 %finish.1 = (bf16[1,128,4096]{2,1,0:T(8,128)(2,1)}, f32[1,2,128]{2,1,0:T(2,128)}, bf16[2,512,256]{2,1,0:T(8,128)(2,1)}, bf16[2,256,512]{2,1,0:T(8,128)(2,1)}) custom-call(bf16[2,4,4,16,128]{4,3,2,1,0:T(8,128)(2,1)} %get-tuple-element.9.rows_hbm, bf16[128,16]{1,0:T(8,128)(2,1)} %get-tuple-element.10.unpick_hbm, f32[1,2,128]{2,1,0:T(2,128)} %get-tuple-element.11.gate_hbm, ...), custom_call_target="tpu_custom_call" | custom-call | tf_op jit(solution)/shard_map/finish/pallas_call | solution.py:571

commit v7 on v6

--- a/solution.py
+++ b/solution.py
@@ -295,14 +295,14 @@
     step(1, 0)
     own_rows[1].forward()
 
+    step(0, 3)
+    step(0, 1)
+    own_rows[0].last()
     @pl.when(away)
     def _():
         cross.wait_recv()
 
     all_rows.first()
-    step(0, 3)
-    step(0, 1)
-    own_rows[0].last()
     step(1, 3)
     step(0, 2)
     own_rows[1].last()
@@ -329,22 +329,27 @@
         outs.append(cp)
 
     def slot_part(k):
-        @pl.loop(0, NX)
-        def _(i):
-            for j in range(NY):
-                part = dot(win[k, wide(i * NY + j), :], zb[1, r, k], 1, 1).astype(BF)
-                for h in range(2):
-                    ps[k, h, i, j] = part[h * COL : (h + 1) * COL]
-
-        pair[k] = send(ps.at[k, oc], rsib.at[k], sib)
+        pair[k] = []
+        for n in range(2):
+
+            @pl.loop(2 * n, 2 * n + 2)
+            def _(i):
+                for j in range(NY):
+                    part = dot(win[k, wide(i * NY + j), :], zb[1, r, k], 1, 1).astype(BF)
+                    for h in range(2):
+                        ps[k, h, i, j] = part[h * COL : (h + 1) * COL]
+
+            at = slice(2 * n, 2 * n + 2)
+            pair[k].append(send(ps.at[k, oc, at], rsib.at[k, at], sib))
 
     def pair_sum(k):
-        pair[k].wait_recv()
-
-        @pl.loop(0, NX)
-        def _(i):
-            for j in range(NY):
-                ps[k, c, i, j] = (ps[k, c, i, j].astype(F32) + rsib[k, i, j].astype(F32)).astype(BF)
+        for n in range(2):
+            pair[k][n].wait_recv()
+
+            @pl.loop(2 * n, 2 * n + 2)
+            def _(i):
+                for j in range(NY):
+                    ps[k, c, i, j] = (ps[k, c, i, j].astype(F32) + rsib[k, i, j].astype(F32)).astype(BF)
 
         for d in (1, 3, 2):
             if k == 0:
@@ -435,19 +440,27 @@
         ]
         return jnp.concatenate(blocks, axis=1)
 
+    zstep(0, 5)
+    all_rows.done()
+    for k in range(2):
+        for j in range(2):
+            at = slice(j * 2 * COL, (j + 1) * 2 * COL)
+            dwout_ref[k, :, at] = dot(factor(0, k), columns(1, k, j), 0, 0).astype(BF)
+    leave(dwout_ref, dwout_hbm)
     zstep(1, 5)
-    all_rows.done()
     for k in range(2):
         for j in range(2):
             at = slice(j * 2 * COL, (j + 1) * 2 * COL)
             dwin_ref[k, at, :] = dot(columns(0, k, j), factor(1, k), 0, 0).astype(BF)
     leave(dwin_ref, dwin_hbm)
-    zstep(0, 5)
-    for k in range(2):
-        for j in range(2):
-            at = slice(j * 2 * COL, (j + 1) * 2 * COL)
-            dwout_ref[k, :, at] = dot(factor(0, k), columns(1, k, j), 0, 0).astype(BF)
-    leave(dwout_ref, dwout_hbm)
+
+    assert counter[0] <= NSEM, counter[0]
+    for cp in sent + forth:
+        cp.wait_send()
+
+    @pl.when(away)
+    def _():
+        cross.wait_send()
 
     for cp in kept["back"]:
         cp.wait_recv()
@@ -460,18 +473,10 @@
 
     leave(rows_out, rows_hbm)
 
-    assert counter[0] <= NSEM, counter[0]
-    for cp in sent:
-        cp.wait_send()
-
-    for cp in forth + kept["back"]:
+    for cp in kept["back"]:
         cp.wait_send()
     for cp in outs:
         cp.wait()
-
-    @pl.when(away)
-    def _():
-        cross.wait_send()
 
 
 def finish(

time: 70.2 us -> 69.6 us (level)
  no operation moved by 1% of the time
where the time goes in v7:
time: 69.6 us; the launch traced here: 69.4 us
  Pallas kernels  68.8 us (99%)
    pallas_call x1, Pallas kernels, local(): pl.pallas_call(kernel, out_shape=(jax.ShapeDtypeStruct((2, NX, NY, ROWS,...  66.2 us
    pallas_call x1, Pallas kernels, local(): pl.pallas_call(finish, out_shape=(jax.ShapeDtypeStruct((1, TOK, D), BF),...  2.52 us

profile of v7, /device:TPU:1, one launch (start us, length us, event | category | flops | bytes accessed | tf_op | source)
XLA Modules:
  0.0 69.4 jit_solution(4127228796769623470)
XLA Ops:
  0.6 66.2 %expert_backward.1 = (bf16[2,4,4,16,128]{4,3,2,1,0:T(8,128)(2,1)}, bf16[128,16]{1,0:T(8,128)(2,1)}, f32[1,2,128]{2,1,0:T(2,128)}, bf16[2,512,256]{2,1,0:T(8,128)(2,1)}, bf16[2,256,512]{2,1,0:T(8,128)(2,1)}) custom-call(bf16[1,128,4096]{2,1,0:T(8,128)(2,1)} %tok_hbm.1, bf16[1,128,4096]{2,1,0:T(8,128)(2,1)} %grad_hbm.1, f32[1,2,128]{2,1,0:T(2,128)} %gates_ref.1, ...), custom_call_target="tpu_custom_call" | custom-call | tf_op jit(solution)/shard_map/expert_backward/pallas_call | solution.py:522
  66.9 2.5 %finish.1 = (bf16[1,128,4096]{2,1,0:T(8,128)(2,1)}, f32[1,2,128]{2,1,0:T(2,128)}, bf16[2,512,256]{2,1,0:T(8,128)(2,1)}, bf16[2,256,512]{2,1,0:T(8,128)(2,1)}) custom-call(bf16[2,4,4,16,128]{4,3,2,1,0:T(8,128)(2,1)} %get-tuple-element.9.rows_hbm, bf16[128,16]{1,0:T(8,128)(2,1)} %get-tuple-element.10.unpick_hbm, f32[1,2,128]{2,1,0:T(2,128)} %get-tuple-element.11.gate_hbm, ...), custom_call_target="tpu_custom_call" | custom-call | tf_op jit(solution)/shard_map/finish/pallas_call | solution.py:576

commit v8 on v7

--- a/solution.py
+++ b/solution.py
@@ -132,24 +132,21 @@
         pick += dot(a, b)
     pick = pick.astype(BF)
 
-    loads[0].wait()
-    loads[1].wait()
+    def wide(p):
+        return pl.ds(pl.multiple_of(turned(p) * 2 * COL, 2 * COL), 2 * COL)
+
+    for a, source in enumerate((tok, grad)):
+        loads[a].wait()
+
+        @pl.loop(0, NX)
+        def _(i):
+            for j in range(NY):
+                packed = dot(pick, source[:, wide(i * NY + j)]).astype(BF)
+                for k in range(2):
+                    pk[k, i, j, a] = packed[:, k * COL : (k + 1) * COL]
+
     loads[2].start()
     loads[3].start()
-
-    def wide(p):
-        return pl.ds(pl.multiple_of(turned(p) * 2 * COL, 2 * COL), 2 * COL)
-
-    @pl.loop(0, NX)
-    def _(i):
-        for j in range(NY):
-            cols = wide(i * NY + j)
-            xr = dot(pick, tok[:, cols]).astype(BF)
-            dr = dot(pick, grad[:, cols]).astype(BF)
-            for k in range(2):
-                pk[k, i, j, 0] = xr[:, k * COL : (k + 1) * COL]
-                pk[k, i, j, 1] = dr[:, k * COL : (k + 1) * COL]
-
     pl.semaphore_wait(barrier, PLANE - 1 + NZ - 1)
 
 

time: 69.6 us -> 69.7 us (level)
  no operation moved by 1% of the time
where the time goes in v8:
time: 69.7 us; the launch traced here: 69.5 us
  Pallas kernels  68.9 us (99%)
    pallas_call x1, Pallas kernels, local(): pl.pallas_call(kernel, out_shape=(jax.ShapeDtypeStruct((2, NX, NY, ROWS,...  66.4 us
    pallas_call x1, Pallas kernels, local(): pl.pallas_call(finish, out_shape=(jax.ShapeDtypeStruct((1, TOK, D), BF),...  2.52 us

profile of v8, /device:TPU:1, one launch (start us, length us, event | category | flops | bytes accessed | tf_op | source)
XLA Modules:
  0.0 69.5 jit_solution(13198573755195012167)
XLA Ops:
  0.6 66.4 %expert_backward.1 = (bf16[2,4,4,16,128]{4,3,2,1,0:T(8,128)(2,1)}, bf16[128,16]{1,0:T(8,128)(2,1)}, f32[1,2,128]{2,1,0:T(2,128)}, bf16[2,512,256]{2,1,0:T(8,128)(2,1)}, bf16[2,256,512]{2,1,0:T(8,128)(2,1)}) custom-call(bf16[1,128,4096]{2,1,0:T(8,128)(2,1)} %tok_hbm.1, bf16[1,128,4096]{2,1,0:T(8,128)(2,1)} %grad_hbm.1, f32[1,2,128]{2,1,0:T(2,128)} %gates_ref.1, ...), custom_call_target="tpu_custom_call" | custom-call | tf_op jit(solution)/shard_map/expert_backward/pallas_call | solution.py:519
  67.0 2.5 %finish.1 = (bf16[1,128,4096]{2,1,0:T(8,128)(2,1)}, f32[1,2,128]{2,1,0:T(2,128)}, bf16[2,512,256]{2,1,0:T(8,128)(2,1)}, bf16[2,256,512]{2,1,0:T(8,128)(2,1)}) custom-call(bf16[2,4,4,16,128]{4,3,2,1,0:T(8,128)(2,1)} %get-tuple-element.9.rows_hbm, bf16[128,16]{1,0:T(8,128)(2,1)} %get-tuple-element.10.unpick_hbm, f32[1,2,128]{2,1,0:T(2,128)} %get-tuple-element.11.gate_hbm, ...), custom_call_target="tpu_custom_call" | custom-call | tf_op jit(solution)/shard_map/finish/pallas_call | solution.py:573
